TPU v7x, 512 devices: a whole 4x4x16 slice. The times are simulated.
512 devices in a mesh: rep: 64 (over z, y_hi, core), fsdp: 8 (over y_lo, x).
Axes of the slice: x: 4, y: 4 (y_hi: 2, y_lo: 2; y = y_hi * 2 + y_lo), z: 16, core: 2. Of those that a mesh axis runs over, the one named last changes fastest.
Arguments:
- anchor: float32 [256, 4096], P('fsdp'), may hold values from -3 to 3
- inner_weights: bfloat16 [64, 256, 4096], P('rep', 'fsdp'), may hold values from -300 to 300
- momentum: float32 [256, 4096], P('fsdp'), may hold values from -1.5 to 1.5
- adam_first: float32 [64, 256, 4096], P('rep', 'fsdp'), may hold values from -1.5 to 1.5
- adam_second: float32 [64, 256, 4096], P('rep', 'fsdp'), may hold values from 0.01 to 1
Outputs:
- new_anchor: float32 [256, 4096], P('fsdp')
- new_momentum: float32 [256, 4096], P('fsdp')
- new_inner: bfloat16 [64, 256, 4096], P('rep', 'fsdp')
- new_first: float32 [64, 256, 4096], P('rep', 'fsdp')
- new_second: float32 [64, 256, 4096], P('rep', 'fsdp')
All inputs are finite; a program needn't handle non-finite values.
Results may differ from a plain program's by a relative error of at most 0.012.
Values sent between devices are 32-bit elements; how exact they have to be, the bound alone decides.
No kernel may reach another device: no remote copies, remote signals or barrier semaphores. Data moves between devices by JAX's collectives and lax.ppermute only.
A program may use at most 64 MiB of HBM per device.

v0:
```python
import jax
import jax.numpy as jnp
from jax import lax
from jax.sharding import PartitionSpec as P

OUTER_MOMENTUM = 0.9
OUTER_RATE = 0.7
MIX_KEEP = 0.5
CLIP_RMS = 0.1
EPSILON = 1e-06


def clip_grad(outer_grad, mean_square):
    clip_factor = jnp.minimum(1.0, CLIP_RMS / jnp.sqrt(mean_square + EPSILON))
    return clip_factor * outer_grad


def per_device(anchor, inner_weights, momentum, adam_first, adam_second):
    replica_count = lax.axis_size("rep")
    entries_total = anchor.shape[0] * lax.axis_size("fsdp") * anchor.shape[1]
    inner_float = inner_weights[0].astype(jnp.float32)
    pseudo_grad = (anchor - inner_float).astype(jnp.bfloat16)
    grad_total, first_total, second_total = lax.psum(
        (pseudo_grad.astype(jnp.float32), adam_first[0], adam_second[0]), "rep"
    )
    outer_grad = grad_total / replica_count
    local_sum = jnp.sum(outer_grad * outer_grad)
    mean_square = lax.psum(local_sum, "fsdp") / entries_total
    clipped = clip_grad(outer_grad, mean_square)
    first_mean = first_total / replica_count
    second_mean = second_total / replica_count
    new_momentum = OUTER_MOMENTUM * momentum + clipped
    new_anchor = anchor - OUTER_RATE * (clipped + OUTER_MOMENTUM * new_momentum)
    new_inner = (MIX_KEEP * inner_float + (1.0 - MIX_KEEP) * new_anchor).astype(jnp.bfloat16)
    new_first = MIX_KEEP * adam_first[0] + (1.0 - MIX_KEEP) * first_mean
    new_second = MIX_KEEP * adam_second[0] + (1.0 - MIX_KEEP) * second_mean
    return (new_anchor, new_momentum, new_inner[None], new_first[None], new_second[None])


def solution(mesh):
    placed = (
        P("fsdp", None),
        P("rep", "fsdp", None),
        P("fsdp", None),
        P("rep", "fsdp", None),
        P("rep", "fsdp", None),
    )
    return jax.shard_map(
        per_device,
        mesh=mesh,
        in_specs=placed,
        out_specs=(
            P("fsdp", None),
            P("fsdp", None),
            P("rep", "fsdp", None),
            P("rep", "fsdp", None),
            P("rep", "fsdp", None),
        ),
        check_vma=False,
    )
```

profile of v0, /device:TPU:1, one launch (start us, length us, event | category | flops | bytes accessed | tf_op | source)
XLA Modules:
  0.0 577.8 jit_solution(2495786348471007147)
XLA Ops:
  7.2 0.0 all-reduce.3.cloned.1.call-start
  7.2 1.9 fusion.4
  9.2 0.0 copy-start.1
  9.2 0.0 all-reduce.3.cloned.1.call-update
  9.2 0.0 copy-start
  9.2 540.1 %all-reduce.3.cloned.1.call-done = (f32[32,4096]{1,0:T(8,128)}, f32[32,4096]{1,0:T(8,128)}, f32[32,4096]{1,0:T(8,128)}) async-done(((f32[32,4096]{1,0:T(8,128)}, f32[32,4096]{1,0:T(8,128)}, f32[32,4096]{1,0:T(8,128)}), (f32[32,4096]{1,0:T(8,128)}, f32[32,4096]{1,0:T(8,128)}, f32[32,4096]{1,0:T(8,128)})) %all-reduce.3.cloned.1.call-update) | async-done | bytes 1572880 | tf_op jit(solution)/shard_map/psum | solution.py:23
  549.3 1.8 multiply_reduce_fusion
  551.1 15.6 %psum.29 = f32[]{:T(128)} all-reduce(f32[]{:T(128)} %multiply_reduce_fusion), channel_id=1, replica_groups=mesh['rep'=64,'fsdp'=8] {'fsdp'}, use_global_device_ids=true, to_apply=%region_2.0 | all-reduce | flops 1 | bytes 8 | tf_op jit(solution)/shard_map/psum | solution.py:28
  567.3 0.0 copy-done.1
  567.3 0.0 copy-done
  567.3 0.0 copy-start.2
  567.3 0.0 copy-start.3
  567.4 0.0 copy-start.4
  567.4 0.0 copy-start.5
  567.4 2.4 add_bitcast_fusion
  569.8 0.0 copy-done.2
  569.8 0.0 copy-done.3
  569.8 0.0 copy-done.4
  569.8 0.0 copy-done.5
  569.8 1.2 fusion.3
Async XLA Ops:
  7.2 542.1 %all-reduce.3.cloned.1.call-start = ((), (), s32[]{:S(2)}) async-start(), calls=%async_computation | async-start | bytes 3145728 | tf_op jit(solution)/shard_map/psum | solution.py:23
  9.2 558.2 %copy-start.1 = (f32[1,32,4096]{2,1,0:T(8,128)S(1)}, f32[1,32,4096]{2,1,0:T(8,128)}, u32[]{:S(2)}) copy-start(f32[1,32,4096]{2,1,0:T(8,128)} %param.9) | copy-start | bytes 1572868
  9.2 558.1 %copy-start = (f32[1,32,4096]{2,1,0:T(8,128)S(1)}, f32[1,32,4096]{2,1,0:T(8,128)}, u32[]{:S(2)}) copy-start(f32[1,32,4096]{2,1,0:T(8,128)} %param.8) | copy-start | bytes 1572868
  567.3 2.5 copy-start.2
  567.3 2.4 copy-start.3
  567.4 2.4 copy-start.4
  567.4 2.4 copy-start.5
Sparse Core Ops, SparseCore 0:
  11.7 537.5 all-reduce.2
where the time goes:
time: 580 us; the launch traced here: 578 us
  waiting for transfers between devices  540 us (93%)
  blocking collectives  15.6 us (3%)
  between operations  14.8 us (3%)
  other arithmetic  7.32 us (1%)
    psum x1, waiting for transfers between devices, per_device(): lax.psum((pseudo_grad.astype(jnp.float32), adam_first[0], adam_second[0])...  540 us
    psum x1, blocking collectives, per_device(): mean_square = lax.psum(local_sum, 'fsdp') / entries_total  15.6 us
  transfers between devices with their start and end apart: 1, of which 1 were waited for; matrix products, arithmetic and copies ran while one was open for 0% of the time, Pallas kernels for 0%

commit v1 on v0

v1 whole, which is shorter than its diff:
```python
import jax
import jax.numpy as jnp
from jax import lax
from jax.sharding import Mesh, PartitionSpec as P

OUTER_MOMENTUM = 0.9
OUTER_RATE = 0.7
MIX_KEEP = 0.5
CLIP_RMS = 0.1
EPSILON = 1e-06

AXES = ("z", "yh", "c", "yl", "x")
SIZES = (16, 2, 2, 2, 4)
REP = ("z", "yh", "c")
FSDP = ("yl", "x")
N_Z, N_Y, N_C = SIZES[:3]


def scatter_sum(parts, axis):
    return jnp.sum(lax.all_to_all(parts, axis, 0, 0), axis=0)


def gather_parts(part, axis):
    return lax.all_gather(part, axis, axis=0)


def per_device(anchor, inner_weights, momentum, adam_first, adam_second):
    rows, columns = anchor.shape
    replica_count = N_Z * N_Y * N_C
    entries_total = rows * columns * SIZES[3] * SIZES[4]
    inner_float = inner_weights[0].astype(jnp.float32)
    pseudo_grad = (anchor - inner_float).astype(jnp.bfloat16).astype(jnp.float32)
    own_rows = rows // (N_C * N_Y)

    def split(array):
        return array.reshape(N_C, N_Y, own_rows, columns)

    terms = jnp.stack([split(pseudo_grad), split(adam_first[0]), split(adam_second[0])], axis=2)
    terms = scatter_sum(terms, "c")
    terms = scatter_sum(terms, "yh")
    width = columns // N_Z
    terms = terms.reshape(3, own_rows, N_Z, width).transpose(2, 0, 1, 3)
    total = scatter_sum(terms, "z")
    mean = total / replica_count

    spread = lax.all_to_all(jnp.broadcast_to(mean[None], (N_Z,) + mean.shape), "z", 0, 0)
    spread = spread.transpose(1, 2, 0, 3).reshape(3, own_rows, columns)
    spread = gather_parts(spread, "yh")

    def whole(at):
        return gather_parts(spread[:, at], "c").reshape(rows, columns)

    outer_grad, first_mean, second_mean = whole(0), whole(1), whole(2)
    local_sum = jnp.sum(outer_grad * outer_grad)
    sums = lax.all_to_all(jnp.full((SIZES[3] * SIZES[4], 8, 128), local_sum), FSDP, 0, 0)
    mean_square = jnp.sum(sums[:, 0, 0]) / entries_total
    clip_factor = jnp.minimum(1.0, CLIP_RMS / jnp.sqrt(mean_square + EPSILON))
    clipped = clip_factor * outer_grad
    new_momentum = OUTER_MOMENTUM * momentum + clipped
    new_anchor = anchor - OUTER_RATE * (clipped + OUTER_MOMENTUM * new_momentum)
    new_inner = (MIX_KEEP * inner_float + (1.0 - MIX_KEEP) * new_anchor).astype(jnp.bfloat16)
    new_first = MIX_KEEP * adam_first[0] + (1.0 - MIX_KEEP) * first_mean
    new_second = MIX_KEEP * adam_second[0] + (1.0 - MIX_KEEP) * second_mean
    return (new_anchor, new_momentum, new_inner[None], new_first[None], new_second[None])


def solution(mesh):
    fine = Mesh(mesh.devices.reshape(SIZES), AXES)
    shared, own = P(FSDP, None), P(REP, FSDP, None)
    return jax.shard_map(
        per_device,
        mesh=fine,
        in_specs=(shared, own, shared, own, own),
        out_specs=(shared, shared, own, own, own),
        check_vma=False,
    )
```

time: 580 us -> 123 us (0.21)
  waiting for transfers between devices: 540 us -> 1.79 us
  blocking collectives: 15.6 us -> 106 us
  between operations: 14.8 us -> 1.46 us
    psum x1 -> x0, waiting for transfers between devices: 540 us -> none  [per_device(): lax.psum((pseudo_grad.astype(jnp.float32), adam_first[0], adam_second[0])...]
    all_to_all x0 -> x4, blocking collectives: none -> 83.4 us  [the longest x3 52.8 us: scatter_sum(): return jnp.sum(lax.all_to_all(parts, axis, 0, 0), axis=0)]
    all_gather x0 -> x4, blocking collectives: none -> 22.9 us  [gather_parts(): return lax.all_gather(part, axis, axis=0)]
    psum x1 -> x0, blocking collectives: 15.6 us -> none  [per_device(): mean_square = lax.psum(local_sum, 'fsdp') / entries_total]
  transfers between devices with their start and end apart: 1 -> 1, of which waited for: 1 -> 1; matrix products, arithmetic and copies ran while one was open for 0% -> 1% of each run, Pallas kernels for 0% -> 0%
where the time goes in v1:
time: 123 us; the launch traced here: 122 us
  blocking collectives  106 us (86%)
  other arithmetic  5.9 us (5%)
  starting transfers between devices  4.13 us (3%)
  local copies, waits for them, and re-layouts  2.1 us (2%)
  waiting for transfers between devices  1.79 us (1%)
  between operations  1.46 us (1%)
    all_to_all x3, blocking collectives, scatter_sum(): return jnp.sum(lax.all_to_all(parts, axis, 0, 0), axis=0)  52.8 us
    all_to_all x1, blocking collectives, per_device(): lax.all_to_all(jnp.broadcast_to(mean[None], (N_Z,) + mean.shape), 'z', 0, 0)  30.5 us
    all_gather x4, blocking collectives, gather_parts(): return lax.all_gather(part, axis, axis=0)  22.9 us
    all_to_all x1, starting transfers between devices, per_device(): lax.all_to_all(jnp.full((SIZES[3] * SIZES[4], 8, 128), local_sum), FSDP,...  4.13 us
  transfers between devices with their start and end apart: 1, of which 1 were waited for; matrix products, arithmetic and copies ran while one was open for 1% of the time, Pallas kernels for 0%

profile of v1, /device:TPU:1, one launch (start us, length us, event | category | flops | bytes accessed | tf_op | source)
XLA Modules:
  0.0 121.6 jit_solution(8638605097176869224)
XLA Ops:
  0.6 0.0 copy-start.1
  0.6 0.0 copy-start
  0.7 1.2 %fusion = bf16[32,4096]{1,0:T(8,128)(2,1)S(1)} fusion(f32[32,4096]{1,0:T(8,128)} %param.5, bf16[1,32,4096]{2,1,0:T(8,128)(2,1)} %param.6), kind=kLoop, calls=%fused_computation.3 | loop fusion | flops 393216 | bytes 1048576 | tf_op jit(solution)/shard_map/convert_element_type | solution.py:32
  1.9 0.0 copy-done.1
  1.9 0.1 copy-done
  2.1 0.1 pad_maximum_fusion
  2.2 11.5 %all_to_all.25 = f32[2,2,3,8,4096]{4,3,1,2,0:T(8,128)S(1)} all-to-all(f32[2,2,3,8,4096]{4,3,1,2,0:T(8,128)S(1)} %pad_maximum_fusion), channel_id=1, replica_groups=mesh['z'=16,'yh'=2,'c'=2,'yl'=2,'x'=4] {'c'}, dimensions={0} | all-to-all | bytes 3145728 | tf_op jit(solution)/shard_map/all_to_all | solution.py:20
  13.7 0.2 reduce_sum.45
  13.9 0.1 copy.23
  13.9 14.5 %all_to_all.26 = f32[2,3,8,4096]{3,2,1,0:T(8,128)S(1)} all-to-all(f32[2,3,8,4096]{3,2,1,0:T(8,128)S(1)} %copy.23), channel_id=1, replica_groups=mesh['z'=16,'yh'=2,'c'=2,'yl'=2,'x'=4] {'yh'}, dimensions={0} | all-to-all | bytes 1572864 | tf_op jit(solution)/shard_map/all_to_all | solution.py:20
  28.4 0.1 copy.31
  28.6 0.2 copy.24
  28.8 26.8 %all_to_all.27 = f32[16,3,8,256]{3,2,1,0:T(8,128)S(1)} all-to-all(f32[16,3,8,256]{3,2,1,0:T(8,128)S(1)} %copy.24), channel_id=1, replica_groups=mesh['z'=16,'yh'=2,'c'=2,'yl'=2,'x'=4] {'z'}, dimensions={0} | all-to-all | bytes 786432 | tf_op jit(solution)/shard_map/all_to_all | solution.py:20
  55.7 30.5 %all_to_all.28 = f32[16,3,8,256]{3,2,1,0:T(8,128)S(1)} all-to-all(f32[16,3,8,256]{3,2,1,0:T(8,128)S(1)} %broadcast_in_dim.6), channel_id=1, replica_groups=mesh['z'=16,'yh'=2,'c'=2,'yl'=2,'x'=4] {'z'}, dimensions={0} | all-to-all | bytes 786432 | tf_op jit(solution)/shard_map/all_to_all | solution.py:46
  86.3 0.1 copy.25
  86.4 0.1 all_gather_reshape.3
  86.5 8.8 %all_gather.12 = f32[2,3,8,4096]{3,2,1,0:T(8,128)S(1)} all-gather(f32[1,3,8,4096]{3,2,1,0:T(8,128)S(1)} %all_gather_reshape.3), channel_id=1, replica_groups=mesh['z'=16,'yh'=2,'c'=2,'yl'=2,'x'=4] {'yh'}, dimensions={0}, use_global_device_ids=true | all-gather | bytes 1179648 | tf_op jit(solution)/shard_map/all_gather | solution.py:24
  95.3 0.1 fusion.9
  95.4 9.5 %all-gather.2 = f32[4,1,8,4096]{3,2,1,0:T(8,128)S(1)} all-gather(f32[2,1,8,4096]{3,2,1,0:T(8,128)S(1)} %get-tuple-element.8), channel_id=4, replica_groups=mesh['z'=16,'yh'=2,'c'=2,'yl'=2,'x'=4] {'c'}, dimensions={0}, use_global_device_ids=true | all-gather | bytes 786432 | tf_op jit(solution)/shard_map/all_gather | solution.py:24
  104.8 0.9 fusion.3
  105.7 2.2 %all-gather = f32[4,1,8,4096]{3,2,1,0:T(8,128)S(1)} all-gather(f32[2,1,8,4096]{3,2,1,0:T(8,128)S(1)} %get-tuple-element.10), channel_id=2, replica_groups=mesh['z'=16,'yh'=2,'c'=2,'yl'=2,'x'=4] {'c'}, dimensions={0}, use_global_device_ids=true | all-gather | bytes 786432 | tf_op jit(solution)/shard_map/all_gather | solution.py:24
  107.9 0.7 multiply_reduce_fusion
  108.6 1.3 %broadcast_in_dim.7 = f32[8,8,128]{2,1,0:T(8,128)} broadcast(f32[]{:T(128)} %multiply_reduce_fusion), dimensions={} | broadcast | bytes 32772 | tf_op jit(solution)/shard_map/broadcast_in_dim | solution.py:55
  109.9 4.1 %all-to-all-start.4 = ((f32[8,8,128]{2,1,0:T(8,128)}), f32[8,8,128]{2,1,0:T(8,128)S(1)}, u32[]{:S(2)}, u32[]{:S(2)}) async-start(f32[8,8,128]{2,1,0:T(8,128)} %broadcast_in_dim.7), calls=%async_computation.4 | async-start | bytes 65536 | tf_op jit(solution)/shard_map/all_to_all | solution.py:55
  114.0 2.4 %all-gather.1 = f32[4,1,8,4096]{3,2,1,0:T(8,128)S(1)} all-gather(f32[2,1,8,4096]{3,2,1,0:T(8,128)S(1)} %get-tuple-element.9), channel_id=3, replica_groups=mesh['z'=16,'yh'=2,'c'=2,'yl'=2,'x'=4] {'c'}, dimensions={0}, use_global_device_ids=true | all-gather | bytes 786432 | tf_op jit(solution)/shard_map/all_gather | solution.py:24
  116.5 0.9 fusion.4
  117.3 1.8 %all-to-all-done.4 = f32[8,8,128]{2,1,0:T(8,128)S(1)} async-done(((f32[8,8,128]{2,1,0:T(8,128)}), f32[8,8,128]{2,1,0:T(8,128)S(1)}, u32[]{:S(2)}, u32[]{:S(2)}) %all-to-all-start.4) | async-done | bytes 32800 | tf_op jit(solution)/shard_map/all_to_all | solution.py:55
  119.1 0.6 slice_reduce_fusion
  120.4 0.0 copy-done.2
  120.4 0.0 copy-done.3
  120.5 0.0 copy-done.4
  120.5 1.2 fusion.7
  (8 shorter events, 0.2 us)
Async XLA Ops:
  0.6 1.3 %copy-start.1 = (f32[1,32,4096]{2,1,0:T(8,128)S(1)}, f32[1,32,4096]{2,1,0:T(8,128)}, u32[]{:S(2)}) copy-start(f32[1,32,4096]{2,1,0:T(8,128)} %param.8) | copy-start | bytes 1572868
  0.6 1.4 %copy-start = (f32[1,32,4096]{2,1,0:T(8,128)S(1)}, f32[1,32,4096]{2,1,0:T(8,128)}, u32[]{:S(2)}) copy-start(f32[1,32,4096]{2,1,0:T(8,128)} %param.9) | copy-start | bytes 1572868
  107.9 12.6 %copy-start.2 = (f32[32,4096]{1,0:T(8,128)S(1)}, f32[32,4096]{1,0:T(8,128)}, u32[]{:S(2)}) copy-start(f32[32,4096]{1,0:T(8,128)} %param.5) | copy-start | bytes 1572868
  107.9 12.6 %copy-start.3 = (bf16[1,32,4096]{2,1,0:T(8,128)(2,1)S(1)}, bf16[1,32,4096]{2,1,0:T(8,128)(2,1)}, u32[]{:S(2)}) copy-start(bf16[1,32,4096]{2,1,0:T(8,128)(2,1)} %param.6) | copy-start | bytes 786436
  107.9 12.6 %copy-start.4 = (f32[32,4096]{1,0:T(8,128)S(1)}, f32[32,4096]{1,0:T(8,128)}, u32[]{:S(2)}) copy-start(f32[32,4096]{1,0:T(8,128)} %param.7) | copy-start | bytes 1572868
  109.9 9.2 %all-to-all-start.4 = ((f32[8,8,128]{2,1,0:T(8,128)}), f32[8,8,128]{2,1,0:T(8,128)S(1)}, u32[]{:S(2)}, u32[]{:S(2)}) async-start(f32[8,8,128]{2,1,0:T(8,128)} %broadcast_in_dim.7), calls=%async_computation.4 | async-start | bytes 65536 | tf_op jit(solution)/shard_map/all_to_all | solution.py:55

commit v2 on v1

v2 whole, which is shorter than its diff:
```python
import jax
import jax.numpy as jnp
from jax import lax
from jax.sharding import Mesh, PartitionSpec as P

OUTER_MOMENTUM = 0.9
OUTER_RATE = 0.7
MIX_KEEP = 0.5
CLIP_RMS = 0.1
EPSILON = 1e-06

AXES = ("zs", "z1", "yh", "c", "yl", "x")
SIZES = (8, 2, 2, 2, 2, 4)
N_ZS, N_Z1, N_YH, N_C, N_YL, N_X = SIZES
REP = ("zs", "z1", "yh", "c")
NEAR = ("yh", "z1")
FSDP = ("yl", "x")
SWAP = ((0, 1), (1, 0))


def scatter_sum(parts, axis):
    return jnp.sum(lax.all_to_all(parts, axis, 0, 0), axis=0)


def gather_parts(part, axis, count):
    return lax.all_to_all(jnp.broadcast_to(part[None], (count,) + part.shape), axis, 0, 0)


def per_device(anchor, inner_weights, momentum, adam_first, adam_second):
    rows, columns = anchor.shape
    replica_count = N_ZS * N_Z1 * N_YH * N_C
    entries_total = rows * columns * N_YL * N_X
    inner_float = inner_weights[0].astype(jnp.float32)
    pseudo_grad = (anchor - inner_float).astype(jnp.bfloat16).astype(jnp.float32)
    block = (rows // (N_C * N_YH), columns // (N_Z1 * N_ZS))

    def split(array):
        array = array.reshape(N_C, N_YH, block[0], N_Z1 * N_ZS, block[1])
        return array.transpose(0, 1, 3, 2, 4).reshape((N_C, N_YH * N_Z1, N_ZS) + block)

    def join(blocks):
        blocks = blocks.reshape((N_C, N_YH, N_Z1 * N_ZS) + block)
        return blocks.transpose(0, 1, 3, 2, 4).reshape(rows, columns)

    terms = jnp.stack([split(pseudo_grad), split(adam_first[0]), split(adam_second[0])], axis=3)
    terms = scatter_sum(terms, "c")
    terms = scatter_sum(terms, NEAR)
    mean = scatter_sum(terms, "zs") / replica_count

    spread = gather_parts(mean, "zs", N_ZS)
    half = gather_parts(spread, NEAR, N_YH * N_Z1)
    other = lax.ppermute(half, "c", SWAP)

    own_grad = half[:, :, 0]
    squares = jnp.sum((own_grad * own_grad).reshape(-1, 8, 128), axis=0)
    groups = N_C * N_YL * N_X
    sums = lax.all_to_all(jnp.broadcast_to(squares[None], (groups, 8, 128)), ("c",) + FSDP, 0, 0)
    mean_square = jnp.sum(sums) / entries_total

    first_half = lax.axis_index("c") == 0
    both = jnp.stack([jnp.where(first_half, half, other), jnp.where(first_half, other, half)])
    outer_grad, first_mean, second_mean = (join(both[:, :, :, at]) for at in range(3))
    clip_factor = jnp.minimum(1.0, CLIP_RMS / jnp.sqrt(mean_square + EPSILON))
    clipped = clip_factor * outer_grad
    new_momentum = OUTER_MOMENTUM * momentum + clipped
    new_anchor = anchor - OUTER_RATE * (clipped + OUTER_MOMENTUM * new_momentum)
    new_inner = (MIX_KEEP * inner_float + (1.0 - MIX_KEEP) * new_anchor).astype(jnp.bfloat16)
    new_first = MIX_KEEP * adam_first[0] + (1.0 - MIX_KEEP) * first_mean
    new_second = MIX_KEEP * adam_second[0] + (1.0 - MIX_KEEP) * second_mean
    return (new_anchor, new_momentum, new_inner[None], new_first[None], new_second[None])


def solution(mesh):
    fine = Mesh(mesh.devices.reshape(SIZES), AXES)
    shared, own = P(FSDP, None), P(REP, FSDP, None)
    return jax.shard_map(
        per_device,
        mesh=fine,
        in_specs=(shared, own, shared, own, own),
        out_specs=(shared, shared, own, own, own),
        check_vma=False,
    )
```

time: 123 us -> 109 us (0.89); the launches traced: 122 us -> 109 us
  blocking collectives: 106 us -> 82.8 us
  starting transfers between devices: 4.13 us -> 12.4 us
  waiting for transfers between devices: 1.79 us -> 5.86 us
    all_gather x4 -> x0, blocking collectives: 22.9 us -> none  [gather_parts(): return lax.all_gather(part, axis, axis=0)]
    ppermute x0 -> x1, starting transfers between devices: none -> 7.87 us  [per_device(): other = lax.ppermute(half, 'c', SWAP)]
    all_to_all x1, waiting for transfers between devices: 1.79 us -> 5.86 us  [per_device(): lax.all_to_all(jnp.broadcast_to(squares[None], (groups, 8, 128)), ('c',)...]
    all_to_all x3, blocking collectives: 52.8 us -> 51 us  [scatter_sum(): return jnp.sum(lax.all_to_all(parts, axis, 0, 0), axis=0)]
    all_to_all x1 -> x2, blocking collectives: 30.5 us -> 31.8 us  [gather_parts(): lax.all_to_all(jnp.broadcast_to(part[None], (count,) + part.shape), axis,...]
  transfers between devices with their start and end apart: 1 -> 2, of which waited for: 1 -> 1; matrix products, arithmetic and copies ran while one was open for 1% -> 1% of each run, Pallas kernels for 0% -> 0%
where the time goes in v2:
time: 109 us
  blocking collectives  82.8 us (76%)
  starting transfers between devices  12.4 us (11%)
  waiting for transfers between devices  5.86 us (5%)
  other arithmetic  4.94 us (5%)
  local copies, waits for them, and re-layouts  1.51 us (1%)
  between operations  1.5 us (1%)
    all_to_all x3, blocking collectives, scatter_sum(): return jnp.sum(lax.all_to_all(parts, axis, 0, 0), axis=0)  51 us
    all_to_all x2, blocking collectives, gather_parts(): lax.all_to_all(jnp.broadcast_to(part[None], (count,) + part.shape), axis,...  31.8 us
    ppermute x1, starting transfers between devices, per_device(): other = lax.ppermute(half, 'c', SWAP)  7.87 us
    all_to_all x1, waiting for transfers between devices, per_device(): lax.all_to_all(jnp.broadcast_to(squares[None], (groups, 8, 128)), ('c',)...  5.86 us
    all_to_all x1, starting transfers between devices, per_device(): lax.all_to_all(jnp.broadcast_to(squares[None], (groups, 8, 128)), ('c',)...  4.54 us
  transfers between devices with their start and end apart: 2, of which 1 were waited for; matrix products, arithmetic and copies ran while one was open for 1% of the time, Pallas kernels for 0%

profile of v2, /device:TPU:1, one launch (start us, length us, event | category | flops | bytes accessed | tf_op | source)
XLA Modules:
  0.0 109.0 jit_solution(1002285637105966773)
XLA Ops:
  0.6 0.0 copy-start.2
  0.6 0.0 copy-start.1
  0.7 1.2 %fusion = bf16[32,4096]{1,0:T(8,128)(2,1)S(1)} fusion(f32[32,4096]{1,0:T(8,128)} %param.5, bf16[1,32,4096]{2,1,0:T(8,128)(2,1)} %param.6), kind=kLoop, calls=%fused_computation.9 | loop fusion | flops 393216 | bytes 1048576 | tf_op jit(solution)/shard_map/convert_element_type | solution.py:34
  1.9 0.0 copy-done.2
  2.0 0.1 copy-done.1
  2.1 0.1 pad_maximum_fusion
  2.2 11.5 %all_to_all.30 = f32[2,4,8,3,8,256]{5,4,2,1,3,0:T(8,128)S(1)} all-to-all(f32[2,4,8,3,8,256]{5,4,2,1,3,0:T(8,128)S(1)} %pad_maximum_fusion), channel_id=1, replica_groups=mesh['zs'=8,'z1'=2,'yh'=2,'c'=2,'yl'=2,'x'=4] {'c'}, dimensions={0} | all-to-all | bytes 3145728 | tf_op jit(solution)/shard_map/all_to_all | solution.py:22
  13.7 0.2 reduce_sum.45
  13.9 0.1 copy.23
  14.0 14.6 %all_to_all.31 = f32[4,8,3,8,256]{4,3,1,2,0:T(8,128)S(1)} all-to-all(f32[4,8,3,8,256]{4,3,1,2,0:T(8,128)S(1)} %copy.23), channel_id=1, replica_groups=mesh['zs'=8,'z1'=2,'yh'=2,'c'=2,'yl'=2,'x'=4] {'yh','z1'}, dimensions={0} | all-to-all | bytes 1572864 | tf_op jit(solution)/shard_map/all_to_all | solution.py:22
  28.6 0.1 reduce_sum.46
  28.7 24.9 %all_to_all.32 = f32[8,3,8,256]{3,2,1,0:T(8,128)S(1)} all-to-all(f32[8,3,8,256]{3,2,1,0:T(8,128)S(1)} %copy.25), channel_id=1, replica_groups=mesh['zs'=8,'z1'=2,'yh'=2,'c'=2,'yl'=2,'x'=4] {'zs'}, dimensions={0} | all-to-all | bytes 393216 | tf_op jit(solution)/shard_map/all_to_all | solution.py:22
  53.6 20.1 %all_to_all.33 = f32[8,3,8,256]{3,2,1,0:T(8,128)S(1)} all-to-all(f32[8,3,8,256]{3,2,1,0:T(8,128)S(1)} %broadcast_in_dim.8), channel_id=1, replica_groups=mesh['zs'=8,'z1'=2,'yh'=2,'c'=2,'yl'=2,'x'=4] {'zs'}, dimensions={0} | all-to-all | bytes 393216 | tf_op jit(solution)/shard_map/all_to_all | solution.py:26
  73.7 0.1 broadcast_in_dim.9
  73.8 11.7 %all_to_all.34 = f32[4,8,3,8,256]{4,3,1,2,0:T(8,128)S(1)} all-to-all(f32[4,8,3,8,256]{4,3,1,2,0:T(8,128)S(1)} %broadcast_in_dim.9), channel_id=1, replica_groups=mesh['zs'=8,'z1'=2,'yh'=2,'c'=2,'yl'=2,'x'=4] {'yh','z1'}, dimensions={0} | all-to-all | bytes 1572864 | tf_op jit(solution)/shard_map/all_to_all | solution.py:26
  85.5 7.9 %collective-permute-start = (f32[4,8,3,8,256]{4,3,1,2,0:T(8,128)S(1)}, f32[4,8,3,8,256]{4,3,1,2,0:T(8,128)S(1)}, u32[]{:S(2)}, u32[]{:S(2)}) collective-permute-start(f32[4,8,3,8,256]{4,3,1,2,0:T(8,128)S(1)} %all_to_all.34), channel_id=1, source_target_pairs={{0,8},{8,0},{1,9},{9,1},{2,10},{10,2},{3,11},{11,3},{4,12},{12,4},... | collective-permute-start | bytes 2359304 | tf_op jit(solution)/shard_map/ppermute | solution.py:52
  93.4 0.1 reduce_sum.48
  93.5 0.6 broadcast_in_dim.10
  94.1 4.5 %all-to-all-start.5 = ((f32[16,8,128]{2,1,0:T(8,128)}), f32[16,8,128]{2,1,0:T(8,128)S(1)}, u32[]{:S(2)}, u32[]{:S(2)}) async-start(f32[16,8,128]{2,1,0:T(8,128)} %broadcast_in_dim.10), calls=%async_computation.5 | async-start | bytes 131072 | tf_op jit(solution)/shard_map/all_to_all | solution.py:57
  98.7 5.9 %all-to-all-done.5 = f32[16,8,128]{2,1,0:T(8,128)S(1)} async-done(((f32[16,8,128]{2,1,0:T(8,128)}), f32[16,8,128]{2,1,0:T(8,128)S(1)}, u32[]{:S(2)}, u32[]{:S(2)}) %all-to-all-start.5) | async-done | bytes 65568 | tf_op jit(solution)/shard_map/all_to_all | solution.py:57
  104.5 0.6 reduce_sum.49
  105.8 0.0 collective-permute-done
  105.8 0.2 select_bitcast_fusion
  106.0 0.2 pad_maximum_fusion.1
  106.2 0.0 copy-start
  106.2 0.0 copy-start.3
  106.2 0.0 copy-start.4
  106.2 1.1 add_multiply_fusion
  107.3 0.0 copy-done
  107.3 0.2 copy-done.3
  107.5 0.4 copy-done.4
  107.8 1.2 %fusion.6 = (bf16[1,32,4096]{2,1,0:T(8,128)(2,1)}, f32[32,4096]{1,0:T(8,128)}, f32[32,4096]{1,0:T(8,128)}) fusion(bf16[1,32,4096]{2,1,0:T(8,128)(2,1)S(1)} %copy-done.3, f32[32,4096]{1,0:T(8,128)S(1)} %copy-done, f32[32,4096]{1,0:T(8,128)S(1)} %bitcast.47, f32[32,4096]{1,0:T(8,128)S(1)} %copy-done.4), kind=kLoop, calls=%fused_computation.20 | loop fusion | flops 1310720 | bytes 3145728 | tf_op jit(solution)/shard_map/broadcast_in_dim | solution.py:70
  (8 shorter events, 0.1 us)
Async XLA Ops:
  0.6 1.3 %copy-start.2 = (f32[1,32,4096]{2,1,0:T(8,128)S(1)}, f32[1,32,4096]{2,1,0:T(8,128)}, u32[]{:S(2)}) copy-start(f32[1,32,4096]{2,1,0:T(8,128)} %param.8) | copy-start | bytes 1572868
  0.6 1.4 %copy-start.1 = (f32[1,32,4096]{2,1,0:T(8,128)S(1)}, f32[1,32,4096]{2,1,0:T(8,128)}, u32[]{:S(2)}) copy-start(f32[1,32,4096]{2,1,0:T(8,128)} %param.9) | copy-start | bytes 1572868
  85.5 20.4 %collective-permute-start = (f32[4,8,3,8,256]{4,3,1,2,0:T(8,128)S(1)}, f32[4,8,3,8,256]{4,3,1,2,0:T(8,128)S(1)}, u32[]{:S(2)}, u32[]{:S(2)}) collective-permute-start(f32[4,8,3,8,256]{4,3,1,2,0:T(8,128)S(1)} %all_to_all.34), channel_id=1, source_target_pairs={{0,8},{8,0},{1,9},{9,1},{2,10},{10,2},{3,11},{11,3},{4,12},{12,4},... | collective-permute-start | bytes 2359304 | tf_op jit(solution)/shard_map/ppermute | solution.py:52
  94.1 10.4 %all-to-all-start.5 = ((f32[16,8,128]{2,1,0:T(8,128)}), f32[16,8,128]{2,1,0:T(8,128)S(1)}, u32[]{:S(2)}, u32[]{:S(2)}) async-start(f32[16,8,128]{2,1,0:T(8,128)} %broadcast_in_dim.10), calls=%async_computation.5 | async-start | bytes 131072 | tf_op jit(solution)/shard_map/all_to_all | solution.py:57
  106.2 1.1 %copy-start = (f32[32,4096]{1,0:T(8,128)S(1)}, f32[32,4096]{1,0:T(8,128)}, u32[]{:S(2)}) copy-start(f32[32,4096]{1,0:T(8,128)} %param.5) | copy-start | bytes 1572868
  106.2 1.3 %copy-start.3 = (bf16[1,32,4096]{2,1,0:T(8,128)(2,1)S(1)}, bf16[1,32,4096]{2,1,0:T(8,128)(2,1)}, u32[]{:S(2)}) copy-start(bf16[1,32,4096]{2,1,0:T(8,128)(2,1)} %param.6) | copy-start | bytes 786436
  106.2 1.6 %copy-start.4 = (f32[32,4096]{1,0:T(8,128)S(1)}, f32[32,4096]{1,0:T(8,128)}, u32[]{:S(2)}) copy-start(f32[32,4096]{1,0:T(8,128)} %param.7) | copy-start | bytes 1572868

commit v3 on v2

--- a/solution.py
+++ b/solution.py
@@ -42,31 +42,34 @@
         blocks = blocks.reshape((N_C, N_YH, N_Z1 * N_ZS) + block)
         return blocks.transpose(0, 1, 3, 2, 4).reshape(rows, columns)
 
-    terms = jnp.stack([split(pseudo_grad), split(adam_first[0]), split(adam_second[0])], axis=3)
-    terms = scatter_sum(terms, "c")
+    first_core = lax.axis_index("c") == 0
+    blocks = jnp.stack([split(pseudo_grad), split(adam_first[0]), split(adam_second[0])], axis=3)
+    away = jnp.where(first_core, blocks[1], blocks[0])
+    kept = jnp.where(first_core, blocks[0], blocks[1])
+    terms = kept + lax.ppermute(away, "c", SWAP)
     terms = scatter_sum(terms, NEAR)
     mean = scatter_sum(terms, "zs") / replica_count
 
     spread = gather_parts(mean, "zs", N_ZS)
     half = gather_parts(spread, NEAR, N_YH * N_Z1)
+    own_grad = half[:, :, 0]
+    squares = jnp.sum(jnp.sum((own_grad * own_grad).reshape(-1, 8, 128), axis=0), axis=0, keepdims=True)
+    parts = jnp.broadcast_to(squares[None], (N_C * N_YL * N_X, 1, 128))
+    parts, half = lax.optimization_barrier((parts, half))
+    sums = lax.all_to_all(parts, ("c",) + FSDP, 0, 0)
     other = lax.ppermute(half, "c", SWAP)
 
-    own_grad = half[:, :, 0]
-    squares = jnp.sum((own_grad * own_grad).reshape(-1, 8, 128), axis=0)
-    groups = N_C * N_YL * N_X
-    sums = lax.all_to_all(jnp.broadcast_to(squares[None], (groups, 8, 128)), ("c",) + FSDP, 0, 0)
+    both = jnp.stack([jnp.where(first_core, half, other), jnp.where(first_core, other, half)])
+    outer_grad, first_mean, second_mean = (join(both[:, :, :, at]) for at in range(3))
+    new_first = MIX_KEEP * adam_first[0] + (1.0 - MIX_KEEP) * first_mean
+    new_second = MIX_KEEP * adam_second[0] + (1.0 - MIX_KEEP) * second_mean
+    sums, new_first, new_second = lax.optimization_barrier((sums, new_first, new_second))
     mean_square = jnp.sum(sums) / entries_total
-
-    first_half = lax.axis_index("c") == 0
-    both = jnp.stack([jnp.where(first_half, half, other), jnp.where(first_half, other, half)])
-    outer_grad, first_mean, second_mean = (join(both[:, :, :, at]) for at in range(3))
     clip_factor = jnp.minimum(1.0, CLIP_RMS / jnp.sqrt(mean_square + EPSILON))
     clipped = clip_factor * outer_grad
     new_momentum = OUTER_MOMENTUM * momentum + clipped
     new_anchor = anchor - OUTER_RATE * (clipped + OUTER_MOMENTUM * new_momentum)
     new_inner = (MIX_KEEP * inner_float + (1.0 - MIX_KEEP) * new_anchor).astype(jnp.bfloat16)
-    new_first = MIX_KEEP * adam_first[0] + (1.0 - MIX_KEEP) * first_mean
-    new_second = MIX_KEEP * adam_second[0] + (1.0 - MIX_KEEP) * second_mean
     return (new_anchor, new_momentum, new_inner[None], new_first[None], new_second[None])
 
 

time: 109 us -> 106 us (0.972)
  blocking collectives: 82.8 us -> 71.3 us
  starting transfers between devices: 12.4 us -> 21.2 us
  other arithmetic: 4.94 us -> 6.15 us
    all_to_all x3 -> x2, blocking collectives: 51 us -> 39.5 us  [scatter_sum(): return jnp.sum(lax.all_to_all(parts, axis, 0, 0), axis=0)]
    ppermute x0 -> x1, starting transfers between devices: none -> 8.79 us  [per_device(): terms = kept + lax.ppermute(away, 'c', SWAP)]
    all_to_all x1, waiting for transfers between devices: 5.86 us -> 2.95 us  [per_device(): sums = lax.all_to_all(parts, ('c',) + FSDP, 0, 0)]
    ppermute x0 -> x1, waiting for transfers between devices: none -> 1.89 us  [per_device(): terms = kept + lax.ppermute(away, 'c', SWAP)]
  transfers between devices with their start and end apart: 2 -> 3, of which waited for: 1 -> 2; matrix products, arithmetic and copies ran while one was open for 1% -> 2% of each run, Pallas kernels for 0% -> 0%
where the time goes in v3:
time: 106 us
  blocking collectives  71.3 us (67%)
  starting transfers between devices  21.2 us (20%)
  other arithmetic  6.15 us (6%)
  waiting for transfers between devices  4.84 us (5%)
  between operations  1.52 us (1%)
    all_to_all x2, blocking collectives, scatter_sum(): return jnp.sum(lax.all_to_all(parts, axis, 0, 0), axis=0)  39.5 us
    all_to_all x2, blocking collectives, gather_parts(): lax.all_to_all(jnp.broadcast_to(part[None], (count,) + part.shape), axis,...  31.8 us
    ppermute x1, starting transfers between devices, per_device(): terms = kept + lax.ppermute(away, 'c', SWAP)  8.79 us
    ppermute x1, starting transfers between devices, per_device(): other = lax.ppermute(half, 'c', SWAP)  7.87 us
    all_to_all x1, starting transfers between devices, per_device(): sums = lax.all_to_all(parts, ('c',) + FSDP, 0, 0)  4.56 us
    all_to_all x1, waiting for transfers between devices, per_device(): sums = lax.all_to_all(parts, ('c',) + FSDP, 0, 0)  2.95 us
  transfers between devices with their start and end apart: 3, of which 2 were waited for; matrix products, arithmetic and copies ran while one was open for 2% of the time, Pallas kernels for 0%

profile of v3, /device:TPU:1, one launch (start us, length us, event | category | flops | bytes accessed | tf_op | source)
XLA Modules:
  0.0 105.9 jit_solution(8324356755767062416)
XLA Ops:
  0.6 0.0 copy-start.2
  0.6 0.0 copy-start.1
  0.7 1.2 %fusion = bf16[32,4096]{1,0:T(8,128)(2,1)S(1)} fusion(f32[32,4096]{1,0:T(8,128)} %param.5, bf16[1,32,4096]{2,1,0:T(8,128)(2,1)} %param.6), kind=kLoop, calls=%fused_computation.11 | loop fusion | flops 393216 | bytes 1048576 | tf_op jit(solution)/shard_map/convert_element_type | solution.py:34
  1.9 0.0 copy-done.2
  2.0 0.1 copy-done.1
  2.1 0.1 pad_maximum_fusion
  2.2 0.1 select_bitcast_fusion.2
  2.3 8.8 %collective-permute-start = (f32[4,8,3,8,256]{4,3,1,2,0:T(8,128)S(1)}, f32[4,8,3,8,256]{4,3,1,2,0:T(8,128)S(1)}, u32[]{:S(2)}, u32[]{:S(2)}) collective-permute-start(f32[4,8,3,8,256]{4,3,1,2,0:T(8,128)S(1)} %select_bitcast_fusion.2), channel_id=1, source_target_pairs={{0,8},{8,0},{1,9},{9,1},{2,10},{10,2},{3,11},{11,3},{4,12},{12,4},... | collective-permute-start | bytes 2359304 | tf_op jit(solution)/shard_map/ppermute | solution.py:49
  11.1 1.9 %collective-permute-done = f32[4,8,3,8,256]{4,3,1,2,0:T(8,128)S(1)} collective-permute-done((f32[4,8,3,8,256]{4,3,1,2,0:T(8,128)S(1)}, f32[4,8,3,8,256]{4,3,1,2,0:T(8,128)S(1)}, u32[]{:S(2)}, u32[]{:S(2)}) %collective-permute-start) | collective-permute-done | bytes 786464 | tf_op jit(solution)/shard_map/ppermute | solution.py:49
  13.0 0.2 bitcast_add_fusion
  13.2 14.6 %all_to_all.25 = f32[4,8,3,8,256]{4,3,1,2,0:T(8,128)S(1)} all-to-all(f32[4,8,3,8,256]{4,3,1,2,0:T(8,128)S(1)} %bitcast_add_fusion), channel_id=1, replica_groups=mesh['zs'=8,'z1'=2,'yh'=2,'c'=2,'yl'=2,'x'=4] {'yh','z1'}, dimensions={0} | all-to-all | bytes 1572864 | tf_op jit(solution)/shard_map/all_to_all | solution.py:22
  27.8 0.1 reduce_sum.40
  27.9 24.9 %all_to_all.26 = f32[8,3,8,256]{3,2,1,0:T(8,128)S(1)} all-to-all(f32[8,3,8,256]{3,2,1,0:T(8,128)S(1)} %copy.18), channel_id=1, replica_groups=mesh['zs'=8,'z1'=2,'yh'=2,'c'=2,'yl'=2,'x'=4] {'zs'}, dimensions={0} | all-to-all | bytes 393216 | tf_op jit(solution)/shard_map/all_to_all | solution.py:22
  52.9 20.1 %all_to_all.27 = f32[8,3,8,256]{3,2,1,0:T(8,128)S(1)} all-to-all(f32[8,3,8,256]{3,2,1,0:T(8,128)S(1)} %broadcast_in_dim.12), channel_id=1, replica_groups=mesh['zs'=8,'z1'=2,'yh'=2,'c'=2,'yl'=2,'x'=4] {'zs'}, dimensions={0} | all-to-all | bytes 393216 | tf_op jit(solution)/shard_map/all_to_all | solution.py:26
  73.0 0.1 broadcast_in_dim.13
  73.0 11.7 %all_to_all.28 = f32[4,8,3,8,256]{4,3,1,2,0:T(8,128)S(1)} all-to-all(f32[4,8,3,8,256]{4,3,1,2,0:T(8,128)S(1)} %broadcast_in_dim.13), channel_id=1, replica_groups=mesh['zs'=8,'z1'=2,'yh'=2,'c'=2,'yl'=2,'x'=4] {'yh','z1'}, dimensions={0} | all-to-all | bytes 1572864 | tf_op jit(solution)/shard_map/all_to_all | solution.py:26
  84.8 0.1 reduce_sum.42
  84.9 0.6 broadcast_in_dim.28
  85.5 7.9 %collective-permute-start.1 = (f32[4,8,3,8,256]{4,3,1,2,0:T(8,128)S(1)}, f32[4,8,3,8,256]{4,3,1,2,0:T(8,128)}, u32[]{:S(2)}, u32[]{:S(2)}) collective-permute-start(f32[4,8,3,8,256]{4,3,1,2,0:T(8,128)S(1)} %all_to_all.28), channel_id=1, source_target_pairs={{0,8},{8,0},{1,9},{9,1},{2,10},{10,2},{3,11},{11,3},{4,12},{12,4},... | collective-permute-start | bytes 2359304 | tf_op jit(solution)/shard_map/ppermute | solution.py:60
  93.3 4.6 %all-to-all-start.4 = ((f32[16,1,128]{2,1,0:T(1,128)}), f32[16,1,128]{2,1,0:T(1,128)S(1)}, u32[]{:S(2)}, u32[]{:S(2)}) async-start(f32[16,1,128]{2,1,0:T(1,128)} %broadcast_in_dim.28), calls=%async_computation.4 | async-start | bytes 16384 | tf_op jit(solution)/shard_map/all_to_all | solution.py:59
  97.9 0.0 collective-permute-done.1
  97.9 1.3 %select_bitcast_fusion.1 = (f32[1,4,8,3,8,256]{5,4,2,3,1,0:T(8,128)S(1)}, f32[1,4,8,3,8,256]{5,4,2,3,1,0:T(8,128)S(1)}) fusion(f32[4,8,3,8,256]{4,3,1,2,0:T(8,128)S(1)} %all_to_all.28, f32[4,8,3,8,256]{4,3,1,2,0:T(8,128)} %collective-permute-done.1, pred[]{:T(512)S(6)} %eq.3), kind=kLoop, calls=%fused_computation.7 | loop fusion | flops 393216 | bytes 3145729 | tf_op jit(solution)/shard_map/stack | solution.py:62
  99.2 0.1 fusion.3
  99.3 1.1 %fusion.6 = (f32[32,4096]{1,0:T(8,128)}, f32[32,4096]{1,0:T(8,128)}) fusion(f32[32,4096]{1,0:T(8,128)S(1)} %bitcast.59, f32[1,32,4096]{2,1,0:T(8,128)S(1)} %copy-done.1, f32[32,4096]{1,0:T(8,128)S(1)} %bitcast.60, f32[1,32,4096]{2,1,0:T(8,128)S(1)} %copy-done.2), kind=kLoop, calls=%fused_computation.19 | loop fusion | flops 524288 | bytes 3145728 | tf_op jit(solution)/shard_map/add | solution.py:65
  100.4 0.0 copy-start
  100.4 0.0 copy-start.3
  100.4 3.0 %all-to-all-done.4 = f32[16,1,128]{2,1,0:T(1,128)S(1)} async-done(((f32[16,1,128]{2,1,0:T(1,128)}), f32[16,1,128]{2,1,0:T(1,128)S(1)}, u32[]{:S(2)}, u32[]{:S(2)}) %all-to-all-start.4) | async-done | bytes 8224 | tf_op jit(solution)/shard_map/all_to_all | solution.py:59
  103.3 0.6 reduce_sum.43
  104.7 0.0 copy-done
  104.7 0.0 copy-done.3
  104.7 0.0 copy-done.4
  104.7 1.2 %fusion.8 = (bf16[1,32,4096]{2,1,0:T(8,128)(2,1)}, f32[32,4096]{1,0:T(8,128)}, f32[32,4096]{1,0:T(8,128)}) fusion(bf16[1,32,4096]{2,1,0:T(8,128)(2,1)S(1)} %copy-done.3, f32[32,4096]{1,0:T(8,128)S(1)} %copy-done, f32[32,4096]{1,0:T(8,128)S(1)} %bitcast.58, f32[32,4096]{1,0:T(8,128)S(1)} %copy-done.4), kind=kLoop, calls=%fused_computation.24 | loop fusion | flops 1310720 | bytes 3145728 | tf_op jit(solution)/shard_map/broadcast_in_dim | solution.py:73
  (10 shorter events, 0.2 us)
Async XLA Ops:
  0.6 1.3 %copy-start.2 = (f32[1,32,4096]{2,1,0:T(8,128)S(1)}, f32[1,32,4096]{2,1,0:T(8,128)}, u32[]{:S(2)}) copy-start(f32[1,32,4096]{2,1,0:T(8,128)} %param.8) | copy-start | bytes 1572868
  0.6 1.4 %copy-start.1 = (f32[1,32,4096]{2,1,0:T(8,128)S(1)}, f32[1,32,4096]{2,1,0:T(8,128)}, u32[]{:S(2)}) copy-start(f32[1,32,4096]{2,1,0:T(8,128)} %param.9) | copy-start | bytes 1572868
  2.3 10.7 %collective-permute-start = (f32[4,8,3,8,256]{4,3,1,2,0:T(8,128)S(1)}, f32[4,8,3,8,256]{4,3,1,2,0:T(8,128)S(1)}, u32[]{:S(2)}, u32[]{:S(2)}) collective-permute-start(f32[4,8,3,8,256]{4,3,1,2,0:T(8,128)S(1)} %select_bitcast_fusion.2), channel_id=1, source_target_pairs={{0,8},{8,0},{1,9},{9,1},{2,10},{10,2},{3,11},{11,3},{4,12},{12,4},... | collective-permute-start | bytes 2359304 | tf_op jit(solution)/shard_map/ppermute | solution.py:49
  85.5 12.4 %collective-permute-start.1 = (f32[4,8,3,8,256]{4,3,1,2,0:T(8,128)S(1)}, f32[4,8,3,8,256]{4,3,1,2,0:T(8,128)}, u32[]{:S(2)}, u32[]{:S(2)}) collective-permute-start(f32[4,8,3,8,256]{4,3,1,2,0:T(8,128)S(1)} %all_to_all.28), channel_id=1, source_target_pairs={{0,8},{8,0},{1,9},{9,1},{2,10},{10,2},{3,11},{11,3},{4,12},{12,4},... | collective-permute-start | bytes 2359304 | tf_op jit(solution)/shard_map/ppermute | solution.py:60
  93.3 10.0 %all-to-all-start.4 = ((f32[16,1,128]{2,1,0:T(1,128)}), f32[16,1,128]{2,1,0:T(1,128)S(1)}, u32[]{:S(2)}, u32[]{:S(2)}) async-start(f32[16,1,128]{2,1,0:T(1,128)} %broadcast_in_dim.28), calls=%async_computation.4 | async-start | bytes 16384 | tf_op jit(solution)/shard_map/all_to_all | solution.py:59
  100.4 4.3 %copy-start = (f32[32,4096]{1,0:T(8,128)S(1)}, f32[32,4096]{1,0:T(8,128)}, u32[]{:S(2)}) copy-start(f32[32,4096]{1,0:T(8,128)} %param.5) | copy-start | bytes 1572868
  100.4 4.3 %copy-start.3 = (bf16[1,32,4096]{2,1,0:T(8,128)(2,1)S(1)}, bf16[1,32,4096]{2,1,0:T(8,128)(2,1)}, u32[]{:S(2)}) copy-start(bf16[1,32,4096]{2,1,0:T(8,128)(2,1)} %param.6) | copy-start | bytes 786436
  100.4 4.3 %copy-start.4 = (f32[32,4096]{1,0:T(8,128)S(1)}, f32[32,4096]{1,0:T(8,128)}, u32[]{:S(2)}) copy-start(f32[32,4096]{1,0:T(8,128)} %param.7) | copy-start | bytes 1572868

commit v4 on v3

--- a/solution.py
+++ b/solution.py
@@ -57,16 +57,19 @@
     parts = jnp.broadcast_to(squares[None], (N_C * N_YL * N_X, 1, 128))
     parts, half = lax.optimization_barrier((parts, half))
     sums = lax.all_to_all(parts, ("c",) + FSDP, 0, 0)
-    other = lax.ppermute(half, "c", SWAP)
-
-    both = jnp.stack([jnp.where(first_core, half, other), jnp.where(first_core, other, half)])
-    outer_grad, first_mean, second_mean = (join(both[:, :, :, at]) for at in range(3))
+    near_half = N_YH * N_Z1 // 2
+    lower = lax.all_gather(half[:near_half], "c", axis=0)
+    upper = lax.all_gather(half[near_half:], "c", axis=0)
+    both = jnp.concatenate([lower, upper], axis=1)
+    first_mean, second_mean = join(both[:, :, :, 1]), join(both[:, :, :, 2])
     new_first = MIX_KEEP * adam_first[0] + (1.0 - MIX_KEEP) * first_mean
     new_second = MIX_KEEP * adam_second[0] + (1.0 - MIX_KEEP) * second_mean
     sums, new_first, new_second = lax.optimization_barrier((sums, new_first, new_second))
-    mean_square = jnp.sum(sums) / entries_total
+    lanes = jnp.sum(sums, axis=0)
+    total = jnp.dot(lanes, jnp.ones((lanes.shape[1], block[1]), jnp.float32), precision=lax.Precision.HIGHEST)
+    mean_square = total[0] / entries_total
     clip_factor = jnp.minimum(1.0, CLIP_RMS / jnp.sqrt(mean_square + EPSILON))
-    clipped = clip_factor * outer_grad
+    clipped = join(clip_factor * both[:, :, :, 0])
     new_momentum = OUTER_MOMENTUM * momentum + clipped
     new_anchor = anchor - OUTER_RATE * (clipped + OUTER_MOMENTUM * new_momentum)
     new_inner = (MIX_KEEP * inner_float + (1.0 - MIX_KEEP) * new_anchor).astype(jnp.bfloat16)

time: 106 us -> 104 us (0.981)
  blocking collectives: 71.3 us -> 76 us
  waiting for transfers between devices: 4.84 us -> 1.89 us
  starting transfers between devices: 21.2 us -> 19.2 us
  other arithmetic: 6.15 us -> 4.39 us
    ppermute x1 -> x0, starting transfers between devices: 7.87 us -> none  [per_device(): other = lax.ppermute(half, 'c', SWAP)]
    all_to_all x1, starting transfers between devices: 4.56 us -> 10.4 us  [per_device(): sums = lax.all_to_all(parts, ('c',) + FSDP, 0, 0)]
    all_gather x0 -> x2, blocking collectives: none -> 4.74 us  [the longest x1 2.37 us: per_device(): lower = lax.all_gather(half[:near_half], 'c', axis=0)]
    all_to_all x1, waiting for transfers between devices: 2.95 us -> 0.01 us  [per_device(): sums = lax.all_to_all(parts, ('c',) + FSDP, 0, 0)]
    another operation x2 -> x0, other arithmetic: 1.36 us -> none  [per_device(): jnp.stack([jnp.where(first_core, half, other), jnp.where(first_core, othe...]
  transfers between devices with their start and end apart: 3 -> 2, of which waited for: 2 -> 1; matrix products, arithmetic and copies ran while one was open for 2% -> 1% of each run, Pallas kernels for 0% -> 0%
where the time goes in v4:
time: 104 us
  blocking collectives  76 us (73%)
  starting transfers between devices  19.2 us (18%)
  other arithmetic  4.39 us (4%)
  waiting for transfers between devices  1.89 us (2%)
  local copies, waits for them, and re-layouts  1.22 us (1%)
    all_to_all x2, blocking collectives, scatter_sum(): return jnp.sum(lax.all_to_all(parts, axis, 0, 0), axis=0)  39.5 us
    all_to_all x2, blocking collectives, gather_parts(): lax.all_to_all(jnp.broadcast_to(part[None], (count,) + part.shape), axis,...  31.8 us
    all_to_all x1, starting transfers between devices, per_device(): sums = lax.all_to_all(parts, ('c',) + FSDP, 0, 0)  10.4 us
    ppermute x1, starting transfers between devices, per_device(): terms = kept + lax.ppermute(away, 'c', SWAP)  8.79 us
    all_gather x1, blocking collectives, per_device(): lower = lax.all_gather(half[:near_half], 'c', axis=0)  2.37 us
    all_gather x1, blocking collectives, per_device(): upper = lax.all_gather(half[near_half:], 'c', axis=0)  2.37 us
  transfers between devices with their start and end apart: 2, of which 1 were waited for; matrix products, arithmetic and copies ran while one was open for 1% of the time, Pallas kernels for 0%

profile of v4, /device:TPU:1, one launch (start us, length us, event | category | flops | bytes accessed | tf_op | source)
XLA Modules:
  0.0 103.7 jit_solution(719870806117513310)
XLA Ops:
  0.6 0.0 copy-start.2
  0.6 0.0 copy-start.1
  0.7 1.2 %fusion = bf16[32,4096]{1,0:T(8,128)(2,1)S(1)} fusion(f32[32,4096]{1,0:T(8,128)} %param.5, bf16[1,32,4096]{2,1,0:T(8,128)(2,1)} %param.6), kind=kLoop, calls=%fused_computation.9 | loop fusion | flops 393216 | bytes 1048576 | tf_op jit(solution)/shard_map/convert_element_type | solution.py:34
  1.9 0.0 copy-done.2
  2.0 0.1 copy-done.1
  2.1 0.1 pad_maximum_fusion
  2.2 0.1 select_bitcast_fusion
  2.3 8.8 %collective-permute-start = (f32[4,8,3,8,256]{4,3,1,2,0:T(8,128)S(1)}, f32[4,8,3,8,256]{4,3,1,2,0:T(8,128)S(1)}, u32[]{:S(2)}, u32[]{:S(2)}) collective-permute-start(f32[4,8,3,8,256]{4,3,1,2,0:T(8,128)S(1)} %select_bitcast_fusion), channel_id=1, source_target_pairs={{0,8},{8,0},{1,9},{9,1},{2,10},{10,2},{3,11},{11,3},{4,12},{12,4},... | collective-permute-start | bytes 2359304 | tf_op jit(solution)/shard_map/ppermute | solution.py:49
  11.1 1.9 %collective-permute-done = f32[4,8,3,8,256]{4,3,1,2,0:T(8,128)S(1)} collective-permute-done((f32[4,8,3,8,256]{4,3,1,2,0:T(8,128)S(1)}, f32[4,8,3,8,256]{4,3,1,2,0:T(8,128)S(1)}, u32[]{:S(2)}, u32[]{:S(2)}) %collective-permute-start) | collective-permute-done | bytes 786464 | tf_op jit(solution)/shard_map/ppermute | solution.py:49
  13.0 0.2 bitcast_add_fusion
  13.2 14.6 %all_to_all.25 = f32[4,8,3,8,256]{4,3,1,2,0:T(8,128)S(1)} all-to-all(f32[4,8,3,8,256]{4,3,1,2,0:T(8,128)S(1)} %bitcast_add_fusion), channel_id=1, replica_groups=mesh['zs'=8,'z1'=2,'yh'=2,'c'=2,'yl'=2,'x'=4] {'yh','z1'}, dimensions={0} | all-to-all | bytes 1572864 | tf_op jit(solution)/shard_map/all_to_all | solution.py:22
  27.8 0.1 reduce_sum.40
  27.9 24.9 %all_to_all.26 = f32[8,3,8,256]{3,2,1,0:T(8,128)S(1)} all-to-all(f32[8,3,8,256]{3,2,1,0:T(8,128)S(1)} %copy.17), channel_id=1, replica_groups=mesh['zs'=8,'z1'=2,'yh'=2,'c'=2,'yl'=2,'x'=4] {'zs'}, dimensions={0} | all-to-all | bytes 393216 | tf_op jit(solution)/shard_map/all_to_all | solution.py:22
  52.9 20.1 %all_to_all.27 = f32[8,3,8,256]{3,2,1,0:T(8,128)S(1)} all-to-all(f32[8,3,8,256]{3,2,1,0:T(8,128)S(1)} %broadcast_in_dim.14), channel_id=1, replica_groups=mesh['zs'=8,'z1'=2,'yh'=2,'c'=2,'yl'=2,'x'=4] {'zs'}, dimensions={0} | all-to-all | bytes 393216 | tf_op jit(solution)/shard_map/all_to_all | solution.py:26
  73.0 0.1 broadcast_in_dim.15
  73.0 11.7 %all_to_all.28 = f32[4,8,3,8,256]{4,3,1,2,0:T(8,128)S(1)} all-to-all(f32[4,8,3,8,256]{4,3,1,2,0:T(8,128)S(1)} %broadcast_in_dim.15), channel_id=1, replica_groups=mesh['zs'=8,'z1'=2,'yh'=2,'c'=2,'yl'=2,'x'=4] {'yh','z1'}, dimensions={0} | all-to-all | bytes 1572864 | tf_op jit(solution)/shard_map/all_to_all | solution.py:26
  84.8 0.1 reduce_sum.42
  84.9 0.6 broadcast_in_dim.32
  85.5 10.4 %all-to-all-start.4 = ((f32[16,1,128]{2,1,0:T(1,128)}), f32[16,1,128]{2,1,0:T(1,128)S(1)}, u32[]{:S(2)}, u32[]{:S(2)}) async-start(f32[16,1,128]{2,1,0:T(1,128)} %broadcast_in_dim.32), calls=%async_computation.4 | async-start | bytes 16384 | tf_op jit(solution)/shard_map/all_to_all | solution.py:59
  95.9 0.1 fusion.12
  95.9 2.4 %all-gather = f32[4,8,3,8,256]{4,3,2,1,0:T(8,128)S(1)} all-gather(f32[2,8,3,8,256]{4,3,2,1,0:T(8,128)S(1)} %copy.19), channel_id=2, replica_groups=mesh['zs'=8,'z1'=2,'yh'=2,'c'=2,'yl'=2,'x'=4] {'c'}, dimensions={0}, use_global_device_ids=true | all-gather | bytes 1179648 | tf_op jit(solution)/shard_map/all_gather | solution.py:61
  98.3 2.4 %all-gather.1 = f32[4,8,3,8,256]{4,3,2,1,0:T(8,128)S(1)} all-gather(f32[2,8,3,8,256]{4,3,2,1,0:T(8,128)S(1)} %copy.20), channel_id=3, replica_groups=mesh['zs'=8,'z1'=2,'yh'=2,'c'=2,'yl'=2,'x'=4] {'c'}, dimensions={0}, use_global_device_ids=true | all-gather | bytes 1179648 | tf_op jit(solution)/shard_map/all_gather | solution.py:62
  100.7 0.1 fusion.3
  100.9 0.0 copy-start
  100.9 0.0 copy-start.3
  100.9 0.0 copy-start.4
  100.9 1.1 %fusion.5 = (f32[32,4096]{1,0:T(8,128)}, f32[32,4096]{1,0:T(8,128)}) fusion(f32[32,4096]{1,0:T(8,128)S(1)} %bitcast.66, f32[1,32,4096]{2,1,0:T(8,128)S(1)} %copy-done.1, f32[32,4096]{1,0:T(8,128)S(1)} %bitcast.67, f32[1,32,4096]{2,1,0:T(8,128)S(1)} %copy-done.2), kind=kLoop, calls=%fused_computation.16 | loop fusion | flops 524288 | bytes 3145728 | tf_op jit(solution)/shard_map/add | solution.py:66
  102.0 0.0 all-to-all-done.4
  102.0 0.1 fusion.8
  102.2 0.1 broadcast_multiply_fusion
  102.3 0.2 copy-done.4
  102.5 1.2 %fusion.7 = (bf16[1,32,4096]{2,1,0:T(8,128)(2,1)}, f32[32,4096]{1,0:T(8,128)}, f32[32,4096]{1,0:T(8,128)}) fusion(bf16[1,32,4096]{2,1,0:T(8,128)(2,1)S(1)} %copy-done.3, f32[32,4096]{1,0:T(8,128)S(1)} %copy-done, f32[32,4096]{1,0:T(8,128)S(1)} %bitcast.62, f32[32,4096]{1,0:T(8,128)S(1)} %copy-done.4), kind=kLoop, calls=%fused_computation.21 | loop fusion | flops 1310720 | bytes 3145728 | tf_op jit(solution)/shard_map/broadcast_in_dim | solution.py:76
  (14 shorter events, 0.2 us)
Async XLA Ops:
  0.6 1.3 %copy-start.2 = (f32[1,32,4096]{2,1,0:T(8,128)S(1)}, f32[1,32,4096]{2,1,0:T(8,128)}, u32[]{:S(2)}) copy-start(f32[1,32,4096]{2,1,0:T(8,128)} %param.8) | copy-start | bytes 1572868
  0.6 1.4 %copy-start.1 = (f32[1,32,4096]{2,1,0:T(8,128)S(1)}, f32[1,32,4096]{2,1,0:T(8,128)}, u32[]{:S(2)}) copy-start(f32[1,32,4096]{2,1,0:T(8,128)} %param.9) | copy-start | bytes 1572868
  2.3 10.7 %collective-permute-start = (f32[4,8,3,8,256]{4,3,1,2,0:T(8,128)S(1)}, f32[4,8,3,8,256]{4,3,1,2,0:T(8,128)S(1)}, u32[]{:S(2)}, u32[]{:S(2)}) collective-permute-start(f32[4,8,3,8,256]{4,3,1,2,0:T(8,128)S(1)} %select_bitcast_fusion), channel_id=1, source_target_pairs={{0,8},{8,0},{1,9},{9,1},{2,10},{10,2},{3,11},{11,3},{4,12},{12,4},... | collective-permute-start | bytes 2359304 | tf_op jit(solution)/shard_map/ppermute | solution.py:49
  85.5 16.5 %all-to-all-start.4 = ((f32[16,1,128]{2,1,0:T(1,128)}), f32[16,1,128]{2,1,0:T(1,128)S(1)}, u32[]{:S(2)}, u32[]{:S(2)}) async-start(f32[16,1,128]{2,1,0:T(1,128)} %broadcast_in_dim.32), calls=%async_computation.4 | async-start | bytes 16384 | tf_op jit(solution)/shard_map/all_to_all | solution.py:59
  100.9 1.4 %copy-start = (f32[32,4096]{1,0:T(8,128)S(1)}, f32[32,4096]{1,0:T(8,128)}, u32[]{:S(2)}) copy-start(f32[32,4096]{1,0:T(8,128)} %param.5) | copy-start | bytes 1572868
  100.9 1.4 %copy-start.3 = (bf16[1,32,4096]{2,1,0:T(8,128)(2,1)S(1)}, bf16[1,32,4096]{2,1,0:T(8,128)(2,1)}, u32[]{:S(2)}) copy-start(bf16[1,32,4096]{2,1,0:T(8,128)(2,1)} %param.6) | copy-start | bytes 786436
  100.9 1.6 %copy-start.4 = (f32[32,4096]{1,0:T(8,128)S(1)}, f32[32,4096]{1,0:T(8,128)}, u32[]{:S(2)}) copy-start(f32[32,4096]{1,0:T(8,128)} %param.7) | copy-start | bytes 1572868

commit v5 on v4

--- a/solution.py
+++ b/solution.py
@@ -31,7 +31,7 @@
     replica_count = N_ZS * N_Z1 * N_YH * N_C
     entries_total = rows * columns * N_YL * N_X
     inner_float = inner_weights[0].astype(jnp.float32)
-    pseudo_grad = (anchor - inner_float).astype(jnp.bfloat16).astype(jnp.float32)
+    pseudo_grad = anchor - inner_float
     block = (rows // (N_C * N_YH), columns // (N_Z1 * N_ZS))
 
     def split(array):

time: 104 us -> 104 us (level)
    convert_element_type x1 -> x0, other arithmetic: 1.24 us -> none  [per_device(): (anchor - inner_float).astype(jnp.bfloat16).astype(jnp.float32)]
    sub x0 -> x1, other arithmetic: none -> 1.24 us  [per_device(): pseudo_grad = anchor - inner_float]
where the time goes in v5:
time: 104 us
  blocking collectives  76 us (73%)
  starting transfers between devices  19.2 us (18%)
  other arithmetic  4.35 us (4%)
  waiting for transfers between devices  1.89 us (2%)
  local copies, waits for them, and re-layouts  1.28 us (1%)
    all_to_all x2, blocking collectives, scatter_sum(): return jnp.sum(lax.all_to_all(parts, axis, 0, 0), axis=0)  39.5 us
    all_to_all x2, blocking collectives, gather_parts(): lax.all_to_all(jnp.broadcast_to(part[None], (count,) + part.shape), axis,...  31.8 us
    all_to_all x1, starting transfers between devices, per_device(): sums = lax.all_to_all(parts, ('c',) + FSDP, 0, 0)  10.4 us
    ppermute x1, starting transfers between devices, per_device(): terms = kept + lax.ppermute(away, 'c', SWAP)  8.79 us
    all_gather x1, blocking collectives, per_device(): lower = lax.all_gather(half[:near_half], 'c', axis=0)  2.37 us
    all_gather x1, blocking collectives, per_device(): upper = lax.all_gather(half[near_half:], 'c', axis=0)  2.37 us
  transfers between devices with their start and end apart: 2, of which 1 were waited for; matrix products, arithmetic and copies ran while one was open for 1% of the time, Pallas kernels for 0%

profile of v5, /device:TPU:1, one launch (start us, length us, event | category | flops | bytes accessed | tf_op | source)
XLA Modules:
  0.0 103.7 jit_solution(9302460677204057765)
XLA Ops:
  0.6 0.0 copy-start.2
  0.6 0.0 copy-start.1
  0.7 1.2 %convert_subtract_fusion = f32[32,4096]{1,0:T(8,128)S(1)} fusion(f32[32,4096]{1,0:T(8,128)} %param.5, bf16[1,32,4096]{2,1,0:T(8,128)(2,1)} %param.6), kind=kLoop, calls=%fused_computation.8 | loop fusion | flops 262144 | bytes 1310720 | tf_op jit(solution)/shard_map/sub | solution.py:34
  1.9 0.0 copy-done.2
  1.9 0.2 copy-done.1
  2.1 0.1 pad_maximum_fusion
  2.2 0.1 select_bitcast_fusion
  2.3 8.8 %collective-permute-start = (f32[4,8,3,8,256]{4,3,1,2,0:T(8,128)S(1)}, f32[4,8,3,8,256]{4,3,1,2,0:T(8,128)S(1)}, u32[]{:S(2)}, u32[]{:S(2)}) collective-permute-start(f32[4,8,3,8,256]{4,3,1,2,0:T(8,128)S(1)} %select_bitcast_fusion), channel_id=1, source_target_pairs={{0,8},{8,0},{1,9},{9,1},{2,10},{10,2},{3,11},{11,3},{4,12},{12,4},... | collective-permute-start | bytes 2359304 | tf_op jit(solution)/shard_map/ppermute | solution.py:49
  11.1 1.9 %collective-permute-done = f32[4,8,3,8,256]{4,3,1,2,0:T(8,128)S(1)} collective-permute-done((f32[4,8,3,8,256]{4,3,1,2,0:T(8,128)S(1)}, f32[4,8,3,8,256]{4,3,1,2,0:T(8,128)S(1)}, u32[]{:S(2)}, u32[]{:S(2)}) %collective-permute-start) | collective-permute-done | bytes 786464 | tf_op jit(solution)/shard_map/ppermute | solution.py:49
  13.0 0.2 bitcast_add_fusion
  13.2 14.6 %all_to_all.25 = f32[4,8,3,8,256]{4,3,1,2,0:T(8,128)S(1)} all-to-all(f32[4,8,3,8,256]{4,3,1,2,0:T(8,128)S(1)} %bitcast_add_fusion), channel_id=1, replica_groups=mesh['zs'=8,'z1'=2,'yh'=2,'c'=2,'yl'=2,'x'=4] {'yh','z1'}, dimensions={0} | all-to-all | bytes 1572864 | tf_op jit(solution)/shard_map/all_to_all | solution.py:22
  27.8 0.1 reduce_sum.40
  27.9 24.9 %all_to_all.26 = f32[8,3,8,256]{3,2,1,0:T(8,128)S(1)} all-to-all(f32[8,3,8,256]{3,2,1,0:T(8,128)S(1)} %copy.17), channel_id=1, replica_groups=mesh['zs'=8,'z1'=2,'yh'=2,'c'=2,'yl'=2,'x'=4] {'zs'}, dimensions={0} | all-to-all | bytes 393216 | tf_op jit(solution)/shard_map/all_to_all | solution.py:22
  52.9 20.1 %all_to_all.27 = f32[8,3,8,256]{3,2,1,0:T(8,128)S(1)} all-to-all(f32[8,3,8,256]{3,2,1,0:T(8,128)S(1)} %broadcast_in_dim.14), channel_id=1, replica_groups=mesh['zs'=8,'z1'=2,'yh'=2,'c'=2,'yl'=2,'x'=4] {'zs'}, dimensions={0} | all-to-all | bytes 393216 | tf_op jit(solution)/shard_map/all_to_all | solution.py:26
  73.0 0.1 broadcast_in_dim.15
  73.0 11.7 %all_to_all.28 = f32[4,8,3,8,256]{4,3,1,2,0:T(8,128)S(1)} all-to-all(f32[4,8,3,8,256]{4,3,1,2,0:T(8,128)S(1)} %broadcast_in_dim.15), channel_id=1, replica_groups=mesh['zs'=8,'z1'=2,'yh'=2,'c'=2,'yl'=2,'x'=4] {'yh','z1'}, dimensions={0} | all-to-all | bytes 1572864 | tf_op jit(solution)/shard_map/all_to_all | solution.py:26
  84.8 0.1 reduce_sum.42
  84.9 0.6 broadcast_in_dim.32
  85.5 10.4 %all-to-all-start.4 = ((f32[16,1,128]{2,1,0:T(1,128)}), f32[16,1,128]{2,1,0:T(1,128)S(1)}, u32[]{:S(2)}, u32[]{:S(2)}) async-start(f32[16,1,128]{2,1,0:T(1,128)} %broadcast_in_dim.32), calls=%async_computation.4 | async-start | bytes 16384 | tf_op jit(solution)/shard_map/all_to_all | solution.py:59
  95.9 0.1 fusion.11
  95.9 2.4 %all-gather = f32[4,8,3,8,256]{4,3,2,1,0:T(8,128)S(1)} all-gather(f32[2,8,3,8,256]{4,3,2,1,0:T(8,128)S(1)} %copy.19), channel_id=2, replica_groups=mesh['zs'=8,'z1'=2,'yh'=2,'c'=2,'yl'=2,'x'=4] {'c'}, dimensions={0}, use_global_device_ids=true | all-gather | bytes 1179648 | tf_op jit(solution)/shard_map/all_gather | solution.py:61
  98.3 2.4 %all-gather.1 = f32[4,8,3,8,256]{4,3,2,1,0:T(8,128)S(1)} all-gather(f32[2,8,3,8,256]{4,3,2,1,0:T(8,128)S(1)} %copy.20), channel_id=3, replica_groups=mesh['zs'=8,'z1'=2,'yh'=2,'c'=2,'yl'=2,'x'=4] {'c'}, dimensions={0}, use_global_device_ids=true | all-gather | bytes 1179648 | tf_op jit(solution)/shard_map/all_gather | solution.py:62
  100.7 0.1 fusion.2
  100.9 0.0 copy-start
  100.9 0.0 copy-start.3
  100.9 0.0 copy-start.4
  100.9 1.1 %fusion.4 = (f32[32,4096]{1,0:T(8,128)}, f32[32,4096]{1,0:T(8,128)}) fusion(f32[32,4096]{1,0:T(8,128)S(1)} %bitcast.66, f32[1,32,4096]{2,1,0:T(8,128)S(1)} %copy-done.1, f32[32,4096]{1,0:T(8,128)S(1)} %bitcast.67, f32[1,32,4096]{2,1,0:T(8,128)S(1)} %copy-done.2), kind=kLoop, calls=%fused_computation.15 | loop fusion | flops 524288 | bytes 3145728 | tf_op jit(solution)/shard_map/add | solution.py:66
  102.0 0.0 all-to-all-done.4
  102.0 0.1 fusion.7
  102.2 0.1 broadcast_multiply_fusion
  102.3 0.2 copy-done.4
  102.5 1.2 %fusion.6 = (bf16[1,32,4096]{2,1,0:T(8,128)(2,1)}, f32[32,4096]{1,0:T(8,128)}, f32[32,4096]{1,0:T(8,128)}) fusion(bf16[1,32,4096]{2,1,0:T(8,128)(2,1)S(1)} %copy-done.3, f32[32,4096]{1,0:T(8,128)S(1)} %copy-done, f32[32,4096]{1,0:T(8,128)S(1)} %bitcast.62, f32[32,4096]{1,0:T(8,128)S(1)} %copy-done.4), kind=kLoop, calls=%fused_computation.20 | loop fusion | flops 1310720 | bytes 3145728 | tf_op jit(solution)/shard_map/broadcast_in_dim | solution.py:76
  (13 shorter events, 0.2 us)
Async XLA Ops:
  0.6 1.3 %copy-start.2 = (f32[1,32,4096]{2,1,0:T(8,128)S(1)}, f32[1,32,4096]{2,1,0:T(8,128)}, u32[]{:S(2)}) copy-start(f32[1,32,4096]{2,1,0:T(8,128)} %param.8) | copy-start | bytes 1572868
  0.6 1.4 %copy-start.1 = (f32[1,32,4096]{2,1,0:T(8,128)S(1)}, f32[1,32,4096]{2,1,0:T(8,128)}, u32[]{:S(2)}) copy-start(f32[1,32,4096]{2,1,0:T(8,128)} %param.9) | copy-start | bytes 1572868
  2.3 10.7 %collective-permute-start = (f32[4,8,3,8,256]{4,3,1,2,0:T(8,128)S(1)}, f32[4,8,3,8,256]{4,3,1,2,0:T(8,128)S(1)}, u32[]{:S(2)}, u32[]{:S(2)}) collective-permute-start(f32[4,8,3,8,256]{4,3,1,2,0:T(8,128)S(1)} %select_bitcast_fusion), channel_id=1, source_target_pairs={{0,8},{8,0},{1,9},{9,1},{2,10},{10,2},{3,11},{11,3},{4,12},{12,4},... | collective-permute-start | bytes 2359304 | tf_op jit(solution)/shard_map/ppermute | solution.py:49
  85.5 16.5 %all-to-all-start.4 = ((f32[16,1,128]{2,1,0:T(1,128)}), f32[16,1,128]{2,1,0:T(1,128)S(1)}, u32[]{:S(2)}, u32[]{:S(2)}) async-start(f32[16,1,128]{2,1,0:T(1,128)} %broadcast_in_dim.32), calls=%async_computation.4 | async-start | bytes 16384 | tf_op jit(solution)/shard_map/all_to_all | solution.py:59
  100.9 1.4 %copy-start = (f32[32,4096]{1,0:T(8,128)S(1)}, f32[32,4096]{1,0:T(8,128)}, u32[]{:S(2)}) copy-start(f32[32,4096]{1,0:T(8,128)} %param.5) | copy-start | bytes 1572868
  100.9 1.4 %copy-start.3 = (bf16[1,32,4096]{2,1,0:T(8,128)(2,1)S(1)}, bf16[1,32,4096]{2,1,0:T(8,128)(2,1)}, u32[]{:S(2)}) copy-start(bf16[1,32,4096]{2,1,0:T(8,128)(2,1)} %param.6) | copy-start | bytes 786436
  100.9 1.6 %copy-start.4 = (f32[32,4096]{1,0:T(8,128)S(1)}, f32[32,4096]{1,0:T(8,128)}, u32[]{:S(2)}) copy-start(f32[32,4096]{1,0:T(8,128)} %param.7) | copy-start | bytes 1572868

commit v6 on v5

--- a/solution.py
+++ b/solution.py
@@ -13,7 +13,7 @@
 SIZES = (8, 2, 2, 2, 2, 4)
 N_ZS, N_Z1, N_YH, N_C, N_YL, N_X = SIZES
 REP = ("zs", "z1", "yh", "c")
-NEAR = ("yh", "z1")
+NEAR = ("z1", "yh")
 FSDP = ("yl", "x")
 SWAP = ((0, 1), (1, 0))
 
@@ -32,14 +32,14 @@
     entries_total = rows * columns * N_YL * N_X
     inner_float = inner_weights[0].astype(jnp.float32)
     pseudo_grad = anchor - inner_float
-    block = (rows // (N_C * N_YH), columns // (N_Z1 * N_ZS))
+    block = (rows // (N_C * N_Z1), columns // (N_YH * N_ZS))
 
     def split(array):
-        array = array.reshape(N_C, N_YH, block[0], N_Z1 * N_ZS, block[1])
-        return array.transpose(0, 1, 3, 2, 4).reshape((N_C, N_YH * N_Z1, N_ZS) + block)
+        array = array.reshape(N_C, N_Z1, block[0], N_YH * N_ZS, block[1])
+        return array.transpose(0, 1, 3, 2, 4).reshape((N_C, N_Z1 * N_YH, N_ZS) + block)
 
     def join(blocks):
-        blocks = blocks.reshape((N_C, N_YH, N_Z1 * N_ZS) + block)
+        blocks = blocks.reshape((N_C, N_Z1, N_YH * N_ZS) + block)
         return blocks.transpose(0, 1, 3, 2, 4).reshape(rows, columns)
 
     first_core = lax.axis_index("c") == 0
@@ -51,13 +51,13 @@
     mean = scatter_sum(terms, "zs") / replica_count
 
     spread = gather_parts(mean, "zs", N_ZS)
-    half = gather_parts(spread, NEAR, N_YH * N_Z1)
+    half = gather_parts(spread, NEAR, N_Z1 * N_YH)
     own_grad = half[:, :, 0]
     squares = jnp.sum(jnp.sum((own_grad * own_grad).reshape(-1, 8, 128), axis=0), axis=0, keepdims=True)
     parts = jnp.broadcast_to(squares[None], (N_C * N_YL * N_X, 1, 128))
     parts, half = lax.optimization_barrier((parts, half))
     sums = lax.all_to_all(parts, ("c",) + FSDP, 0, 0)
-    near_half = N_YH * N_Z1 // 2
+    near_half = N_Z1 * N_YH // 2
     lower = lax.all_gather(half[:near_half], "c", axis=0)
     upper = lax.all_gather(half[near_half:], "c", axis=0)
     both = jnp.concatenate([lower, upper], axis=1)

time: 104 us -> 104 us (level)
  no operation moved by 1% of the time
where the time goes in v6:
time: 104 us
  blocking collectives  76.1 us (73%)
  starting transfers between devices  19.3 us (19%)
  other arithmetic  4.35 us (4%)
  waiting for transfers between devices  1.89 us (2%)
  local copies, waits for them, and re-layouts  1.28 us (1%)
    all_to_all x2, blocking collectives, scatter_sum(): return jnp.sum(lax.all_to_all(parts, axis, 0, 0), axis=0)  40.6 us
    all_to_all x2, blocking collectives, gather_parts(): lax.all_to_all(jnp.broadcast_to(part[None], (count,) + part.shape), axis,...  30.8 us
    all_to_all x1, starting transfers between devices, per_device(): sums = lax.all_to_all(parts, ('c',) + FSDP, 0, 0)  10.5 us
    ppermute x1, starting transfers between devices, per_device(): terms = kept + lax.ppermute(away, 'c', SWAP)  8.79 us
    all_gather x1, blocking collectives, per_device(): upper = lax.all_gather(half[near_half:], 'c', axis=0)  2.37 us
    all_gather x1, blocking collectives, per_device(): lower = lax.all_gather(half[:near_half], 'c', axis=0)  2.37 us
  transfers between devices with their start and end apart: 2, of which 1 were waited for; matrix products, arithmetic and copies ran while one was open for 1% of the time, Pallas kernels for 0%

profile of v6, /device:TPU:1, one launch (start us, length us, event | category | flops | bytes accessed | tf_op | source)
XLA Modules:
  0.0 103.9 jit_solution(13687953396330679098)
XLA Ops:
  0.6 0.0 copy-start.2
  0.6 0.0 copy-start.1
  0.7 1.2 %convert_subtract_fusion = f32[32,4096]{1,0:T(8,128)S(1)} fusion(f32[32,4096]{1,0:T(8,128)} %param.5, bf16[1,32,4096]{2,1,0:T(8,128)(2,1)} %param.6), kind=kLoop, calls=%fused_computation.8 | loop fusion | flops 262144 | bytes 1310720 | tf_op jit(solution)/shard_map/sub | solution.py:34
  1.9 0.0 copy-done.2
  1.9 0.2 copy-done.1
  2.1 0.1 pad_maximum_fusion
  2.2 0.1 select_bitcast_fusion
  2.3 8.8 %collective-permute-start = (f32[4,8,3,8,256]{4,3,1,2,0:T(8,128)S(1)}, f32[4,8,3,8,256]{4,3,1,2,0:T(8,128)S(1)}, u32[]{:S(2)}, u32[]{:S(2)}) collective-permute-start(f32[4,8,3,8,256]{4,3,1,2,0:T(8,128)S(1)} %select_bitcast_fusion), channel_id=1, source_target_pairs={{0,8},{8,0},{1,9},{9,1},{2,10},{10,2},{3,11},{11,3},{4,12},{12,4},... | collective-permute-start | bytes 2359304 | tf_op jit(solution)/shard_map/ppermute | solution.py:49
  11.1 1.9 %collective-permute-done = f32[4,8,3,8,256]{4,3,1,2,0:T(8,128)S(1)} collective-permute-done((f32[4,8,3,8,256]{4,3,1,2,0:T(8,128)S(1)}, f32[4,8,3,8,256]{4,3,1,2,0:T(8,128)S(1)}, u32[]{:S(2)}, u32[]{:S(2)}) %collective-permute-start) | collective-permute-done | bytes 786464 | tf_op jit(solution)/shard_map/ppermute | solution.py:49
  13.0 0.2 bitcast_add_fusion
  13.2 14.6 %all_to_all.25 = f32[4,8,3,8,256]{4,3,1,2,0:T(8,128)S(1)} all-to-all(f32[4,8,3,8,256]{4,3,1,2,0:T(8,128)S(1)} %bitcast_add_fusion), channel_id=1, replica_groups=mesh['zs'=8,'z1'=2,'yh'=2,'c'=2,'yl'=2,'x'=4] {'z1','yh'}, dimensions={0} | all-to-all | bytes 1572864 | tf_op jit(solution)/shard_map/all_to_all | solution.py:22
  27.8 0.1 reduce_sum.40
  27.9 25.9 %all_to_all.26 = f32[8,3,8,256]{3,2,1,0:T(8,128)S(1)} all-to-all(f32[8,3,8,256]{3,2,1,0:T(8,128)S(1)} %copy.17), channel_id=1, replica_groups=mesh['zs'=8,'z1'=2,'yh'=2,'c'=2,'yl'=2,'x'=4] {'zs'}, dimensions={0} | all-to-all | bytes 393216 | tf_op jit(solution)/shard_map/all_to_all | solution.py:22
  53.9 19.5 %all_to_all.27 = f32[8,3,8,256]{3,2,1,0:T(8,128)S(1)} all-to-all(f32[8,3,8,256]{3,2,1,0:T(8,128)S(1)} %broadcast_in_dim.14), channel_id=1, replica_groups=mesh['zs'=8,'z1'=2,'yh'=2,'c'=2,'yl'=2,'x'=4] {'zs'}, dimensions={0} | all-to-all | bytes 393216 | tf_op jit(solution)/shard_map/all_to_all | solution.py:26
  73.4 0.1 broadcast_in_dim.15
  73.5 11.3 %all_to_all.28 = f32[4,8,3,8,256]{4,3,1,2,0:T(8,128)S(1)} all-to-all(f32[4,8,3,8,256]{4,3,1,2,0:T(8,128)S(1)} %broadcast_in_dim.15), channel_id=1, replica_groups=mesh['zs'=8,'z1'=2,'yh'=2,'c'=2,'yl'=2,'x'=4] {'z1','yh'}, dimensions={0} | all-to-all | bytes 1572864 | tf_op jit(solution)/shard_map/all_to_all | solution.py:26
  84.8 0.1 reduce_sum.42
  84.9 0.6 broadcast_in_dim.32
  85.5 10.5 %all-to-all-start.4 = ((f32[16,1,128]{2,1,0:T(1,128)}), f32[16,1,128]{2,1,0:T(1,128)S(1)}, u32[]{:S(2)}, u32[]{:S(2)}) async-start(f32[16,1,128]{2,1,0:T(1,128)} %broadcast_in_dim.32), calls=%async_computation.4 | async-start | bytes 16384 | tf_op jit(solution)/shard_map/all_to_all | solution.py:59
  96.0 0.1 fusion.11
  96.1 2.4 %all-gather = f32[4,8,3,8,256]{4,3,2,1,0:T(8,128)S(1)} all-gather(f32[2,8,3,8,256]{4,3,2,1,0:T(8,128)S(1)} %copy.19), channel_id=2, replica_groups=mesh['zs'=8,'z1'=2,'yh'=2,'c'=2,'yl'=2,'x'=4] {'c'}, dimensions={0}, use_global_device_ids=true | all-gather | bytes 1179648 | tf_op jit(solution)/shard_map/all_gather | solution.py:61
  98.5 2.4 %all-gather.1 = f32[4,8,3,8,256]{4,3,2,1,0:T(8,128)S(1)} all-gather(f32[2,8,3,8,256]{4,3,2,1,0:T(8,128)S(1)} %copy.20), channel_id=3, replica_groups=mesh['zs'=8,'z1'=2,'yh'=2,'c'=2,'yl'=2,'x'=4] {'c'}, dimensions={0}, use_global_device_ids=true | all-gather | bytes 1179648 | tf_op jit(solution)/shard_map/all_gather | solution.py:62
  100.9 0.1 fusion.2
  101.0 0.0 copy-start
  101.0 0.0 copy-start.3
  101.0 0.0 copy-start.4
  101.1 1.1 %fusion.4 = (f32[32,4096]{1,0:T(8,128)}, f32[32,4096]{1,0:T(8,128)}) fusion(f32[32,4096]{1,0:T(8,128)S(1)} %bitcast.66, f32[1,32,4096]{2,1,0:T(8,128)S(1)} %copy-done.1, f32[32,4096]{1,0:T(8,128)S(1)} %bitcast.67, f32[1,32,4096]{2,1,0:T(8,128)S(1)} %copy-done.2), kind=kLoop, calls=%fused_computation.15 | loop fusion | flops 524288 | bytes 3145728 | tf_op jit(solution)/shard_map/add | solution.py:66
  102.2 0.0 all-to-all-done.4
  102.2 0.1 fusion.7
  102.4 0.1 broadcast_multiply_fusion
  102.4 0.2 copy-done.4
  102.7 1.2 %fusion.6 = (bf16[1,32,4096]{2,1,0:T(8,128)(2,1)}, f32[32,4096]{1,0:T(8,128)}, f32[32,4096]{1,0:T(8,128)}) fusion(bf16[1,32,4096]{2,1,0:T(8,128)(2,1)S(1)} %copy-done.3, f32[32,4096]{1,0:T(8,128)S(1)} %copy-done, f32[32,4096]{1,0:T(8,128)S(1)} %bitcast.62, f32[32,4096]{1,0:T(8,128)S(1)} %copy-done.4), kind=kLoop, calls=%fused_computation.20 | loop fusion | flops 1310720 | bytes 3145728 | tf_op jit(solution)/shard_map/broadcast_in_dim | solution.py:76
  (13 shorter events, 0.2 us)
Async XLA Ops:
  0.6 1.3 %copy-start.2 = (f32[1,32,4096]{2,1,0:T(8,128)S(1)}, f32[1,32,4096]{2,1,0:T(8,128)}, u32[]{:S(2)}) copy-start(f32[1,32,4096]{2,1,0:T(8,128)} %param.8) | copy-start | bytes 1572868
  0.6 1.4 %copy-start.1 = (f32[1,32,4096]{2,1,0:T(8,128)S(1)}, f32[1,32,4096]{2,1,0:T(8,128)}, u32[]{:S(2)}) copy-start(f32[1,32,4096]{2,1,0:T(8,128)} %param.9) | copy-start | bytes 1572868
  2.3 10.7 %collective-permute-start = (f32[4,8,3,8,256]{4,3,1,2,0:T(8,128)S(1)}, f32[4,8,3,8,256]{4,3,1,2,0:T(8,128)S(1)}, u32[]{:S(2)}, u32[]{:S(2)}) collective-permute-start(f32[4,8,3,8,256]{4,3,1,2,0:T(8,128)S(1)} %select_bitcast_fusion), channel_id=1, source_target_pairs={{0,8},{8,0},{1,9},{9,1},{2,10},{10,2},{3,11},{11,3},{4,12},{12,4},... | collective-permute-start | bytes 2359304 | tf_op jit(solution)/shard_map/ppermute | solution.py:49
  85.5 16.6 %all-to-all-start.4 = ((f32[16,1,128]{2,1,0:T(1,128)}), f32[16,1,128]{2,1,0:T(1,128)S(1)}, u32[]{:S(2)}, u32[]{:S(2)}) async-start(f32[16,1,128]{2,1,0:T(1,128)} %broadcast_in_dim.32), calls=%async_computation.4 | async-start | bytes 16384 | tf_op jit(solution)/shard_map/all_to_all | solution.py:59
  101.0 1.4 %copy-start = (f32[32,4096]{1,0:T(8,128)S(1)}, f32[32,4096]{1,0:T(8,128)}, u32[]{:S(2)}) copy-start(f32[32,4096]{1,0:T(8,128)} %param.5) | copy-start | bytes 1572868
  101.0 1.4 %copy-start.3 = (bf16[1,32,4096]{2,1,0:T(8,128)(2,1)S(1)}, bf16[1,32,4096]{2,1,0:T(8,128)(2,1)}, u32[]{:S(2)}) copy-start(bf16[1,32,4096]{2,1,0:T(8,128)(2,1)} %param.6) | copy-start | bytes 786436
  101.0 1.6 %copy-start.4 = (f32[32,4096]{1,0:T(8,128)S(1)}, f32[32,4096]{1,0:T(8,128)}, u32[]{:S(2)}) copy-start(f32[32,4096]{1,0:T(8,128)} %param.7) | copy-start | bytes 1572868

commit v7 on v6

--- a/solution.py
+++ b/solution.py
@@ -46,7 +46,8 @@
     blocks = jnp.stack([split(pseudo_grad), split(adam_first[0]), split(adam_second[0])], axis=3)
     away = jnp.where(first_core, blocks[1], blocks[0])
     kept = jnp.where(first_core, blocks[0], blocks[1])
-    terms = kept + lax.ppermute(away, "c", SWAP)
+    received, kept_momentum = lax.optimization_barrier((lax.ppermute(away, "c", SWAP), OUTER_MOMENTUM * momentum))
+    terms = kept + received
     terms = scatter_sum(terms, NEAR)
     mean = scatter_sum(terms, "zs") / replica_count
 
@@ -70,7 +71,7 @@
     mean_square = total[0] / entries_total
     clip_factor = jnp.minimum(1.0, CLIP_RMS / jnp.sqrt(mean_square + EPSILON))
     clipped = join(clip_factor * both[:, :, :, 0])
-    new_momentum = OUTER_MOMENTUM * momentum + clipped
+    new_momentum = kept_momentum + clipped
     new_anchor = anchor - OUTER_RATE * (clipped + OUTER_MOMENTUM * new_momentum)
     new_inner = (MIX_KEEP * inner_float + (1.0 - MIX_KEEP) * new_anchor).astype(jnp.bfloat16)
     return (new_anchor, new_momentum, new_inner[None], new_first[None], new_second[None])

time: 104 us -> 108 us (1.038)
  blocking collectives: 76.1 us -> 81.8 us
  starting transfers between devices: 19.3 us -> 13.7 us
  waiting for transfers between devices: 1.89 us -> 5.1 us
    all_gather x1, blocking collectives: 2.37 us -> 8.07 us  [per_device(): lower = lax.all_gather(half[:near_half], 'c', axis=0)]
    all_to_all x1, starting transfers between devices: 10.5 us -> 4.8 us  [per_device(): sums = lax.all_to_all(parts, ('c',) + FSDP, 0, 0)]
    all_to_all x1, waiting for transfers between devices: 0.01 us -> 3.28 us  [per_device(): sums = lax.all_to_all(parts, ('c',) + FSDP, 0, 0)]
  transfers between devices with their start and end apart: 2 -> 2, of which waited for: 1 -> 2; matrix products, arithmetic and copies ran while one was open for 1% -> 1% of each run, Pallas kernels for 0% -> 0%
where the time goes in v7:
time: 108 us
  blocking collectives  81.8 us (76%)
  starting transfers between devices  13.7 us (13%)
  waiting for transfers between devices  5.1 us (5%)
  other arithmetic  4.37 us (4%)
  local copies, waits for them, and re-layouts  1.91 us (2%)
    all_to_all x2, blocking collectives, scatter_sum(): return jnp.sum(lax.all_to_all(parts, axis, 0, 0), axis=0)  40.6 us
    all_to_all x2, blocking collectives, gather_parts(): lax.all_to_all(jnp.broadcast_to(part[None], (count,) + part.shape), axis,...  30.8 us
    ppermute x1, starting transfers between devices, per_device(): lax.ppermute(away, 'c', SWAP)  8.92 us
    all_gather x1, blocking collectives, per_device(): lower = lax.all_gather(half[:near_half], 'c', axis=0)  8.07 us
    all_to_all x1, starting transfers between devices, per_device(): sums = lax.all_to_all(parts, ('c',) + FSDP, 0, 0)  4.8 us
    all_to_all x1, waiting for transfers between devices, per_device(): sums = lax.all_to_all(parts, ('c',) + FSDP, 0, 0)  3.28 us
    all_gather x1, blocking collectives, per_device(): upper = lax.all_gather(half[near_half:], 'c', axis=0)  2.37 us
  transfers between devices with their start and end apart: 2, of which 2 were waited for; matrix products, arithmetic and copies ran while one was open for 1% of the time, Pallas kernels for 0%

profile of v7, /device:TPU:1, one launch (start us, length us, event | category | flops | bytes accessed | tf_op | source)
XLA Modules:
  0.0 107.9 jit_solution(10369288391926777785)
XLA Ops:
  0.6 0.0 copy-start.2
  0.6 0.0 copy-start.1
  0.7 1.2 %convert_subtract_fusion = f32[32,4096]{1,0:T(8,128)S(1)} fusion(f32[32,4096]{1,0:T(8,128)} %param.5, bf16[1,32,4096]{2,1,0:T(8,128)(2,1)} %param.6), kind=kLoop, calls=%fused_computation.8 | loop fusion | flops 262144 | bytes 1310720 | tf_op jit(solution)/shard_map/sub | solution.py:34
  1.9 0.0 copy-done.2
  1.9 0.2 copy-done.1
  2.1 0.1 pad_maximum_fusion
  2.2 0.0 copy-start.5
  2.2 0.1 select_bitcast_fusion
  2.4 8.9 %collective-permute-start = (f32[4,8,3,8,256]{4,3,1,2,0:T(8,128)S(1)}, f32[4,8,3,8,256]{4,3,1,2,0:T(8,128)S(1)}, u32[]{:S(2)}, u32[]{:S(2)}) collective-permute-start(f32[4,8,3,8,256]{4,3,1,2,0:T(8,128)S(1)} %select_bitcast_fusion), channel_id=1, source_target_pairs={{0,8},{8,0},{1,9},{9,1},{2,10},{10,2},{3,11},{11,3},{4,12},{12,4},... | collective-permute-start | bytes 2359304 | tf_op jit(solution)/shard_map/ppermute | solution.py:49
  11.3 0.0 copy-done.5
  11.4 1.8 %collective-permute-done = f32[4,8,3,8,256]{4,3,1,2,0:T(8,128)S(1)} collective-permute-done((f32[4,8,3,8,256]{4,3,1,2,0:T(8,128)S(1)}, f32[4,8,3,8,256]{4,3,1,2,0:T(8,128)S(1)}, u32[]{:S(2)}, u32[]{:S(2)}) %collective-permute-start) | collective-permute-done | bytes 786464 | tf_op jit(solution)/shard_map/ppermute | solution.py:49
  13.2 0.2 bitcast_add_fusion
  13.3 14.6 %all_to_all.25 = f32[4,8,3,8,256]{4,3,1,2,0:T(8,128)S(1)} all-to-all(f32[4,8,3,8,256]{4,3,1,2,0:T(8,128)S(1)} %bitcast_add_fusion), channel_id=1, replica_groups=mesh['zs'=8,'z1'=2,'yh'=2,'c'=2,'yl'=2,'x'=4] {'z1','yh'}, dimensions={0} | all-to-all | bytes 1572864 | tf_op jit(solution)/shard_map/all_to_all | solution.py:22
  28.0 0.1 reduce_sum.40
  28.1 25.9 %all_to_all.26 = f32[8,3,8,256]{3,2,1,0:T(8,128)S(1)} all-to-all(f32[8,3,8,256]{3,2,1,0:T(8,128)S(1)} %copy.17), channel_id=1, replica_groups=mesh['zs'=8,'z1'=2,'yh'=2,'c'=2,'yl'=2,'x'=4] {'zs'}, dimensions={0} | all-to-all | bytes 393216 | tf_op jit(solution)/shard_map/all_to_all | solution.py:22
  54.0 19.5 %all_to_all.27 = f32[8,3,8,256]{3,2,1,0:T(8,128)S(1)} all-to-all(f32[8,3,8,256]{3,2,1,0:T(8,128)S(1)} %broadcast_in_dim.14), channel_id=1, replica_groups=mesh['zs'=8,'z1'=2,'yh'=2,'c'=2,'yl'=2,'x'=4] {'zs'}, dimensions={0} | all-to-all | bytes 393216 | tf_op jit(solution)/shard_map/all_to_all | solution.py:26
  73.6 0.1 broadcast_in_dim.15
  73.6 11.3 %all_to_all.28 = f32[4,8,3,8,256]{4,3,1,2,0:T(8,128)S(1)} all-to-all(f32[4,8,3,8,256]{4,3,1,2,0:T(8,128)S(1)} %broadcast_in_dim.15), channel_id=1, replica_groups=mesh['zs'=8,'z1'=2,'yh'=2,'c'=2,'yl'=2,'x'=4] {'z1','yh'}, dimensions={0} | all-to-all | bytes 1572864 | tf_op jit(solution)/shard_map/all_to_all | solution.py:26
  85.0 0.1 reduce_sum.42
  85.1 0.6 broadcast_in_dim.32
  85.7 0.1 fusion.11
  85.8 8.1 %all-gather = f32[4,8,3,8,256]{4,3,2,1,0:T(8,128)S(1)} all-gather(f32[2,8,3,8,256]{4,3,2,1,0:T(8,128)S(1)} %copy.19), channel_id=2, replica_groups=mesh['zs'=8,'z1'=2,'yh'=2,'c'=2,'yl'=2,'x'=4] {'c'}, dimensions={0}, use_global_device_ids=true | all-gather | bytes 1179648 | tf_op jit(solution)/shard_map/all_gather | solution.py:62
  93.9 2.4 %all-gather.1 = f32[4,8,3,8,256]{4,3,2,1,0:T(8,128)S(1)} all-gather(f32[2,8,3,8,256]{4,3,2,1,0:T(8,128)S(1)} %copy.20), channel_id=3, replica_groups=mesh['zs'=8,'z1'=2,'yh'=2,'c'=2,'yl'=2,'x'=4] {'c'}, dimensions={0}, use_global_device_ids=true | all-gather | bytes 1179648 | tf_op jit(solution)/shard_map/all_gather | solution.py:63
  96.2 4.8 %all-to-all-start.4 = ((f32[16,1,128]{2,1,0:T(1,128)}), f32[16,1,128]{2,1,0:T(1,128)S(1)}, u32[]{:S(2)}, u32[]{:S(2)}) async-start(f32[16,1,128]{2,1,0:T(1,128)} %broadcast_in_dim.32), calls=%async_computation.4 | async-start | bytes 16384 | tf_op jit(solution)/shard_map/all_to_all | solution.py:60
  101.0 0.1 fusion.2
  101.2 0.9 copy-done.3
  102.1 1.1 %fusion.4 = (f32[32,4096]{1,0:T(8,128)}, f32[32,4096]{1,0:T(8,128)}) fusion(f32[32,4096]{1,0:T(8,128)S(1)} %bitcast.66, f32[1,32,4096]{2,1,0:T(8,128)S(1)} %copy-done.1, f32[32,4096]{1,0:T(8,128)S(1)} %bitcast.67, f32[1,32,4096]{2,1,0:T(8,128)S(1)} %copy-done.3), kind=kLoop, calls=%fused_computation.15 | loop fusion | flops 524288 | bytes 3145728 | tf_op jit(solution)/shard_map/add | solution.py:67
  103.2 3.3 %all-to-all-done.4 = f32[16,1,128]{2,1,0:T(1,128)S(1)} async-done(((f32[16,1,128]{2,1,0:T(1,128)}), f32[16,1,128]{2,1,0:T(1,128)S(1)}, u32[]{:S(2)}, u32[]{:S(2)}) %all-to-all-start.4) | async-done | bytes 8224 | tf_op jit(solution)/shard_map/all_to_all | solution.py:60
  106.5 0.1 fusion.7
  106.6 0.1 broadcast_multiply_fusion
  106.7 0.0 copy-done
  106.7 1.2 %fusion.6 = (bf16[1,32,4096]{2,1,0:T(8,128)(2,1)}, f32[32,4096]{1,0:T(8,128)}, f32[32,4096]{1,0:T(8,128)}) fusion(bf16[1,32,4096]{2,1,0:T(8,128)(2,1)S(1)} %copy-done.4, f32[32,4096]{1,0:T(8,128)S(1)} %copy-done, f32[32,4096]{1,0:T(8,128)S(1)} %bitcast.62, f32[32,4096]{1,0:T(8,128)S(1)} %broadcast_multiply_fusion.1), kind=kLoop, calls=%fused_computation.19 | loop fusion | flops 1179648 | bytes 3145728 | tf_op jit(solution)/shard_map/broadcast_in_dim | solution.py:77
  (16 shorter events, 0.3 us)
Async XLA Ops:
  0.6 1.3 %copy-start.2 = (f32[1,32,4096]{2,1,0:T(8,128)S(1)}, f32[1,32,4096]{2,1,0:T(8,128)}, u32[]{:S(2)}) copy-start(f32[1,32,4096]{2,1,0:T(8,128)} %param.8) | copy-start | bytes 1572868
  0.6 1.4 %copy-start.1 = (f32[1,32,4096]{2,1,0:T(8,128)S(1)}, f32[1,32,4096]{2,1,0:T(8,128)}, u32[]{:S(2)}) copy-start(f32[1,32,4096]{2,1,0:T(8,128)} %param.9) | copy-start | bytes 1572868
  2.2 9.1 %copy-start.5 = (f32[32,4096]{1,0:T(8,128)S(1)}, f32[32,4096]{1,0:T(8,128)}, u32[]{:S(2)}) copy-start(f32[32,4096]{1,0:T(8,128)} %param.7) | copy-start | bytes 1572868
  2.4 10.8 %collective-permute-start = (f32[4,8,3,8,256]{4,3,1,2,0:T(8,128)S(1)}, f32[4,8,3,8,256]{4,3,1,2,0:T(8,128)S(1)}, u32[]{:S(2)}, u32[]{:S(2)}) collective-permute-start(f32[4,8,3,8,256]{4,3,1,2,0:T(8,128)S(1)} %select_bitcast_fusion), channel_id=1, source_target_pairs={{0,8},{8,0},{1,9},{9,1},{2,10},{10,2},{3,11},{11,3},{4,12},{12,4},... | collective-permute-start | bytes 2359304 | tf_op jit(solution)/shard_map/ppermute | solution.py:49
  96.2 10.2 %all-to-all-start.4 = ((f32[16,1,128]{2,1,0:T(1,128)}), f32[16,1,128]{2,1,0:T(1,128)S(1)}, u32[]{:S(2)}, u32[]{:S(2)}) async-start(f32[16,1,128]{2,1,0:T(1,128)} %broadcast_in_dim.32), calls=%async_computation.4 | async-start | bytes 16384 | tf_op jit(solution)/shard_map/all_to_all | solution.py:60
  101.0 1.0 copy-start.3
  102.1 4.6 %copy-start = (f32[32,4096]{1,0:T(8,128)S(1)}, f32[32,4096]{1,0:T(8,128)}, u32[]{:S(2)}) copy-start(f32[32,4096]{1,0:T(8,128)} %param.5) | copy-start | bytes 1572868
  102.1 4.6 %copy-start.4 = (bf16[1,32,4096]{2,1,0:T(8,128)(2,1)S(1)}, bf16[1,32,4096]{2,1,0:T(8,128)(2,1)}, u32[]{:S(2)}) copy-start(bf16[1,32,4096]{2,1,0:T(8,128)(2,1)} %param.6) | copy-start | bytes 786436
